TPU v7x, 256 devices: a whole 4x4x8 slice. The times are simulated.
256 devices in a mesh: dp: 16 (over y, x_hi, core), fsdp: 16 (over x_lo, z).
Axes of the slice: x: 4 (x_hi: 2, x_lo: 2; x = x_hi * 2 + x_lo), y: 4, z: 8, core: 2. Of those that a mesh axis runs over, the one named last changes fastest.
Arguments:
- tokens: bfloat16 [2048, 7168], P('fsdp', 'dp'), may hold values from -6 to 6
- cotangent: bfloat16 [2048, 7168], P('fsdp', 'dp'), may hold values from -6 to 6
- gate_codes: bfloat16 [7168, 14336], P('dp', 'fsdp'), may hold values from -127 to 127
- gate_scale: float32 [14336], P('fsdp'), may hold values from 6.471994e-05 to 0.00040449965
- up_codes: bfloat16 [7168, 14336], P('dp', 'fsdp'), may hold values from -127 to 127
- up_scale: float32 [14336], P('fsdp'), may hold values from 6.471994e-05 to 0.00040449965
- down_codes: bfloat16 [14336, 7168], P('fsdp', 'dp'), may hold values from -127 to 127
- down_scale: float32 [1, 7168], P(None, 'dp'), may hold values from 4.576391e-05 to 0.00028602444
Outputs:
- output: bfloat16 [2048, 7168], P('fsdp', 'dp')
- d_tokens: bfloat16 [2048, 7168], P('fsdp', 'dp')
- grad_gate: float32 [7168, 14336], P('dp', 'fsdp')
- grad_up: float32 [7168, 14336], P('dp', 'fsdp')
- grad_down: float32 [14336, 7168], P('fsdp', 'dp')
All inputs are finite; a program needn't handle non-finite values.
Results may differ from a plain program's by a relative error of at most 0.035.
Values may be sent and summed in bfloat16 or wider, within the bound.
A program may use at most 128 MiB of HBM per device.

v0:
```python
import jax
import jax.numpy as jnp
from jax import lax
from jax.sharding import PartitionSpec as P


def dequantize(codes, scale):
    return (codes.astype(jnp.float32) * scale).astype(jnp.bfloat16)


def contract_rows(left, right):
    return lax.dot_general(
        left, right, (((0,), (0,)), ((), ())), preferred_element_type=jnp.float32
    )


def contract_last(left, right):
    return lax.dot_general(
        left, right, (((1,), (1,)), ((), ())), preferred_element_type=jnp.float32
    )


def local(tokens, cotangent, gate_codes, gate_scale, up_codes, up_scale, down_codes, down_scale):
    hidden_width = gate_codes.shape[1]
    weight_both = jnp.concatenate(
        (dequantize(gate_codes, gate_scale[None, :]), dequantize(up_codes, up_scale[None, :])),
        axis=1,
    )
    weight_down = dequantize(down_codes, down_scale)
    tokens_all, cot_all = (
        lax.all_gather(tokens, "fsdp", axis=0, tiled=True),
        lax.all_gather(cotangent, "fsdp", axis=0, tiled=True),
    )
    gate_upper = lax.psum_scatter(
        jnp.dot(tokens_all, weight_both, preferred_element_type=jnp.float32).astype(jnp.bfloat16),
        "dp",
        scatter_dimension=0,
        tiled=True,
    ).astype(jnp.float32)
    gate = gate_upper[:, :hidden_width]
    upper = gate_upper[:, hidden_width:]
    sigmoid_gate = jax.nn.sigmoid(gate)
    activated = gate * sigmoid_gate
    hidden = (activated * upper).astype(jnp.bfloat16)
    hidden_all = lax.all_gather(hidden, "dp", axis=0, tiled=True)
    output = lax.psum_scatter(
        jnp.dot(hidden_all, weight_down, preferred_element_type=jnp.float32).astype(jnp.bfloat16),
        "fsdp",
        scatter_dimension=0,
        tiled=True,
    )
    d_hidden = lax.psum_scatter(
        contract_last(cot_all, weight_down).astype(jnp.bfloat16),
        "dp",
        scatter_dimension=0,
        tiled=True,
    ).astype(jnp.float32)
    d_gate = (d_hidden * upper * sigmoid_gate * (1.0 + gate * (1.0 - sigmoid_gate))).astype(
        jnp.bfloat16
    )
    d_up = (d_hidden * activated).astype(jnp.bfloat16)
    d_both = jnp.concatenate((d_gate, d_up), axis=1)
    d_both_all = lax.all_gather(d_both, "dp", axis=0, tiled=True)
    d_tokens = lax.psum_scatter(
        contract_last(d_both_all, weight_both).astype(jnp.bfloat16),
        "fsdp",
        scatter_dimension=0,
        tiled=True,
    )
    grad_down = contract_rows(hidden_all, cot_all)
    grad_both = contract_rows(tokens_all, d_both_all)
    return (output, d_tokens, grad_both[:, :hidden_width], grad_both[:, hidden_width:], grad_down)


def solution(mesh):
    placed = (
        P("fsdp", "dp"),
        P("fsdp", "dp"),
        P("dp", "fsdp"),
        P("fsdp"),
        P("dp", "fsdp"),
        P("fsdp"),
        P("fsdp", "dp"),
        P(None, "dp"),
    )
    return jax.shard_map(
        local,
        mesh=mesh,
        in_specs=placed,
        out_specs=(
            P("fsdp", "dp"),
            P("fsdp", "dp"),
            P("dp", "fsdp"),
            P("dp", "fsdp"),
            P("fsdp", "dp"),
        ),
        check_vma=False,
    )
```

profile of v0, /device:TPU:1, one launch (start us, length us, event | category | flops | bytes accessed | tf_op | source)
XLA Modules:
  0.0 635.5 jit_solution(1016044841680635359)
XLA Ops:
  7.2 0.0 all-gather.9.cloned.1.call-start
  7.2 0.7 all-gather.9.cloned.1.call-update
  7.9 0.0 all-gather.5.cloned.1.call-start
  7.9 0.7 all-gather.5.cloned.1.call-update
  8.7 0.0 reduce-scatter.17.cloned.1.call-start
  8.7 65.0 %all-gather.9.cloned.1.call-done = bf16[2048,448]{0,1:T(8,128)(2,1)} async-done(((bf16[128,448]{0,1:T(8,128)(2,1)}), bf16[2048,448]{0,1:T(8,128)(2,1)}) %all-gather.9.cloned.1.call-update) | async-done | bytes 1835024 | tf_op jit(solution)/shard_map/all_gather | solution.py:32
  73.7 5.7 convert_bitcast_fusion
  79.5 6.0 copy.17
  85.6 0.0 reduce-scatter.17.cloned.1.call-update
  85.6 0.0 reduce-scatter.13.cloned.1.call-start
  85.6 1.1 copy-done
  86.7 0.2 copy-done.1
  86.9 0.0 copy-done.2
  86.9 0.3 multiply_convert_fusion.1
  87.2 58.3 %all-gather.5.cloned.1.call-done = bf16[2048,448]{0,1:T(8,128)(2,1)} async-done(((bf16[128,448]{0,1:T(8,128)(2,1)}), bf16[2048,448]{0,1:T(8,128)(2,1)}) %all-gather.5.cloned.1.call-update) | async-done | bytes 1835024 | tf_op jit(solution)/shard_map/all_gather | solution.py:31
  145.5 7.7 %fusion = bf16[2048,1792]{0,1:T(8,128)(2,1)} fusion(bf16[2048,448]{0,1:T(8,128)(2,1)} %all-gather.5.cloned.1.call-done, bf16[448,896]{1,0:T(8,128)(2,1)S(1)} %get-tuple-element.10, bf16[448,896]{1,0:T(8,128)(2,1)S(1)} %get-tuple-element.11), kind=kOutput, calls=%fused_computation.1 | convolution fusion | flops 3295215616 | bytes 10780672 | tf_op jit(solution)/shard_map/dot_general | solution.py:35
  153.2 10.0 %copy.13 = bf16[2048,1792]{1,0:T(8,128)(2,1)} copy(bf16[2048,1792]{0,1:T(8,128)(2,1)} %fusion) | data formatting | bytes 14680064
  163.2 0.0 reduce-scatter.13.cloned.1.call-update
  163.2 0.0 all-gather.7.cloned.1.call-start
  163.2 80.2 %reduce-scatter.17.cloned.1.call-done = bf16[128,896]{1,0:T(8,128)(2,1)} async-done(((bf16[2048,896]{1,0:T(8,128)(2,1)}), bf16[128,896]{1,0:T(8,128)(2,1)}) %reduce-scatter.17.cloned.1.call-update) | async-done | bytes 229392
  243.4 1.1 copy.18
  244.5 104.7 %reduce-scatter.13.cloned.1.call-done = bf16[128,1792]{1,0:T(8,128)(2,1)} async-done(((bf16[2048,1792]{1,0:T(8,128)(2,1)}), bf16[128,1792]{1,0:T(8,128)(2,1)}) %reduce-scatter.13.cloned.1.call-update) | async-done | bytes 458768
  349.2 1.3 copy.14
  350.5 0.1 convert_element_type.57
  350.6 0.0 copy-start.5
  350.6 1.0 fusion.3
  351.6 0.0 all-gather.7.cloned.1.call-update
  351.6 0.0 all-gather.11.cloned.1.call-start
  351.6 0.8 pad_maximum_fusion.3
  352.4 0.0 all-gather.11.cloned.1.call-update
  352.5 0.0 reduce-scatter.15.cloned.1.call-start
  352.5 60.2 %all-gather.7.cloned.1.call-done = bf16[2048,896]{0,1:T(8,128)(2,1)} async-done(((bf16[128,896]{0,1:T(8,128)(2,1)}), bf16[2048,896]{0,1:T(8,128)(2,1)}) %all-gather.7.cloned.1.call-update) | async-done | bytes 3670032 | tf_op jit(solution)/shard_map/all_gather | solution.py:45
  412.7 4.4 convolution_convert_fusion.2
  417.2 2.4 copy.15
  419.6 0.0 reduce-scatter.15.cloned.1.call-update
  419.6 0.2 reduce-scatter.19.cloned.1.call-start
  419.8 71.1 %all-gather.11.cloned.1.call-done = bf16[2048,1792]{0,1:T(8,128)(2,1)} async-done(((bf16[128,1792]{0,1:T(8,128)(2,1)}), bf16[2048,1792]{0,1:T(8,128)(2,1)}) %all-gather.11.cloned.1.call-update) | async-done | bytes 7340048 | tf_op jit(solution)/shard_map/all_gather | solution.py:63
  490.9 6.6 %convolution_convert_fusion.1 = bf16[2048,448]{0,1:T(8,128)(2,1)S(1)} fusion(bf16[2048,1792]{0,1:T(8,128)(2,1)} %all-gather.11.cloned.1.call-done, bf16[448,896]{1,0:T(8,128)(2,1)S(1)} %get-tuple-element.10, bf16[448,896]{1,0:T(8,128)(2,1)S(1)} %get-tuple-element.11), kind=kOutput, calls=%fused_computation.4 | convolution fusion | flops 3292463104 | bytes 10780672 | tf_op jit(solution)/shard_map/dot_general | solution.py:18
  497.5 2.5 copy.19
  499.9 0.0 reduce-scatter.19.cloned.1.call-update
  500.0 0.0 copy-start.4
  500.0 6.1 fusion.9
  506.0 47.8 %reduce-scatter.15.cloned.1.call-done = bf16[128,448]{1,0:T(8,128)(2,1)} async-done(((bf16[2048,448]{1,0:T(8,128)(2,1)}), bf16[128,448]{1,0:T(8,128)(2,1)}) %reduce-scatter.15.cloned.1.call-update) | async-done | bytes 114704
  553.8 1.7 copy.16
  555.5 6.6 %convolution_bitcast_fusion = f32[448,1792]{1,0:T(8,128)S(1)} fusion(bf16[2048,1792]{0,1:T(8,128)(2,1)} %all-gather.11.cloned.1.call-done, bf16[2048,448]{0,1:T(8,128)(2,1)S(1)} %copy-done.4), kind=kOutput, calls=%fused_computation.3 | convolution fusion | flops 3288334336 | bytes 12386304 | tf_op jit(solution)/shard_map/dot_general | solution.py:12
  562.1 1.9 fusion.8
  564.0 63.0 %reduce-scatter.19.cloned.1.call-done = bf16[128,448]{1,0:T(8,128)(2,1)} async-done(((bf16[2048,448]{1,0:T(8,128)(2,1)}), bf16[128,448]{1,0:T(8,128)(2,1)}) %reduce-scatter.19.cloned.1.call-update) | async-done | bytes 114704
  627.0 1.7 copy.20
  (7 shorter events, 0.0 us)
Async XLA Ops:
  7.2 66.6 %all-gather.9.cloned.1.call-start = ((), (), s32[]{:S(2)}) async-start(), calls=%async_computation.6 | async-start | bytes 1949696 | tf_op jit(solution)/shard_map/all_gather | solution.py:32
  7.9 137.6 %all-gather.5.cloned.1.call-start = ((), (), s32[]{:S(2)}) async-start(), calls=%async_computation.4 | async-start | bytes 1949696 | tf_op jit(solution)/shard_map/all_gather | solution.py:31
  8.7 234.8 %reduce-scatter.17.cloned.1.call-start = ((), (), s32[]{:S(2)}) async-start(), calls=%async_computation.10 | async-start | bytes 3899392
  85.5 1.1 copy-start
  85.5 1.4 copy-start.1
  85.5 1.4 copy-start.2
  85.5 1.4 copy-start.3
  85.6 263.7 %reduce-scatter.13.cloned.1.call-start = ((), (), s32[]{:S(2)}) async-start(), calls=%async_computation.8 | async-start | bytes 7798784
  163.2 249.6 %all-gather.7.cloned.1.call-start = ((), (), s32[]{:S(2)}) async-start(), calls=%async_computation.5 | async-start | bytes 3899392 | tf_op jit(solution)/shard_map/all_gather | solution.py:45
  350.6 62.2 %copy-start.5 = (f32[1,448]{1,0:T(1,128)S(1)}, f32[1,448]{1,0:T(1,128)}, u32[]{:S(2)}) copy-start(f32[1,448]{1,0:T(1,128)} %param.15) | copy-start | bytes 5380
  351.6 139.3 %all-gather.11.cloned.1.call-start = ((), (), s32[]{:S(2)}) async-start(), calls=%async_computation.7 | async-start | bytes 7798784 | tf_op jit(solution)/shard_map/all_gather | solution.py:63
  352.5 201.3 %reduce-scatter.15.cloned.1.call-start = ((), (), s32[]{:S(2)}) async-start(), calls=%async_computation.9 | async-start | bytes 2228224
  419.6 207.4 %reduce-scatter.19.cloned.1.call-start = ((), (), s32[]{:S(2)}) async-start(), calls=%async_computation.11 | async-start | bytes 2228224
  500.0 55.5 %copy-start.4 = (bf16[2048,448]{0,1:T(8,128)(2,1)S(1)}, bf16[2048,448]{0,1:T(8,128)(2,1)}, u32[]{:S(2)}) copy-start(bf16[2048,448]{0,1:T(8,128)(2,1)} %all-gather.5.cloned.1.call-done) | copy-start | bytes 5505028
Sparse Core Ops, SparseCore 0:
  9.7 63.9 all-gather.8
  75.5 69.9 all-gather.4
  149.9 93.5 reduce-scatter.16
  248.5 100.7 reduce-scatter.12
  352.7 60.0 all-gather.6
  416.2 74.7 all-gather.10
  493.6 60.1 reduce-scatter.14
  556.5 70.4 reduce-scatter.18
where the time goes:
time: 647 us; the launch traced here: 635 us
  waiting for transfers between devices  552 us (85%)
  matrix products  37.1 us (6%)
  local copies, waits for them, and re-layouts  29.8 us (5%)
  between operations  14.2 us (2%)
    unnamed x12, waiting for transfers between devices  297 us
    all_gather x1, waiting for transfers between devices, local(): d_both_all = lax.all_gather(d_both, 'dp', axis=0, tiled=True)  71.1 us
    all_gather x1, waiting for transfers between devices, local(): lax.all_gather(cotangent, 'fsdp', axis=0, tiled=True)  65 us
    all_gather x1, waiting for transfers between devices, local(): hidden_all = lax.all_gather(hidden, 'dp', axis=0, tiled=True)  60.2 us
    all_gather x1, waiting for transfers between devices, local(): lax.all_gather(tokens, 'fsdp', axis=0, tiled=True)  58.3 us
    unnamed x20, local copies, waits for them, and re-layouts  27.9 us
  transfers between devices with their start and end apart: 8, of which 8 were waited for; matrix products, arithmetic and copies ran while one was open for 10% of the time, Pallas kernels for 0%

commit v1 on v0

v1 whole, which is shorter than its diff:
```python
import functools

import jax
import jax.numpy as jnp
from jax import lax
from jax.experimental import pallas as pl
from jax.experimental.pallas import tpu as pltpu
from jax.sharding import PartitionSpec as P

MESH = pl.DeviceIdType.MESH
BF16 = jnp.bfloat16
F32 = jnp.float32

BLOCK = 128
UNIT = 256
UNITS = 8
WIDE = 448
HIDE = 896
FULL = 512
C = 3 * HIDE
ROW = 16
EDGE = FULL - WIDE

ORDER = (
    ("Z", 0), ("M", 0), ("C", 0), ("XL", 0), ("Z", 1), ("M", 1), ("Y1", 0), ("C", 1), ("Z", 4), ("M", 4),
    ("C", 4), ("Z", 2), ("M", 2), ("Y1", 1), ("Y2", 0), ("Z", 5), ("C", 2), ("M", 5), ("Y1", 4), ("Z", 3),
    ("C", 5), ("M", 3), ("Y1", 2), ("Z", 6), ("C", 3), ("M", 6), ("Y2", 1), ("C", 6), ("Y2", 2), ("Z", 7),
    ("Y1", 3), ("M", 7), ("X", 1), ("Y1", 6), ("C", 7), ("Y2", 3), ("Y1", 5), ("Y2", 6), ("X", 3), ("Y1", 7),
    ("X", 6), ("G1", 3), ("Y2", 7), ("X", 2), ("G1", 6), ("X", 7), ("Y2", 5), ("G2", 3), ("G1", 7), ("X", 5),
    ("G3", 3), ("G1", 2), ("G2", 7), ("G2", 6), ("G4", 3), ("K", 3), ("G2", 2), ("G1", 5), ("Y2", 4),
    ("G3", 7), ("G4", 7), ("K", 7), ("G3", 2), ("G1", 1), ("G3", 6), ("G4", 2), ("X", 4), ("G2", 5),
    ("G4", 6), ("K", 6), ("G1", 4), ("G2", 1), ("K", 2), ("X", 0), ("W", 7), ("G3", 5), ("W", 3), ("G2", 4),
    ("G1", 0), ("G4", 5), ("K", 5), ("G3", 1), ("W", 2), ("G4", 1), ("G3", 4), ("K", 1), ("G2", 0), ("W", 5),
    ("G4", 4), ("K", 4), ("W", 4), ("G3", 0), ("W", 1), ("G4", 0), ("K", 0), ("KI", 1), ("W", 0), ("W", 6),
    ("KI", 0),
)
KINDS = ("XL", "Z", "M", "C", "Y1", "Y2", "X", "G1", "G2", "G3", "G4", "W", "K", "KI")


def dot(left, right):
    return jnp.dot(left, right, preferred_element_type=F32)


def kernel(
    tokens_t, cotangent_t, gate_codes, gate_scale, up_codes, up_scale, down_codes_t, down_scale,
    output_t, d_tokens_t, grad_gate, grad_up, grad_down_t,
    own, toks, w_in, w_out, part, core_in, y_raw, y_sum, pair, pair_in, acts, outs, chain_in, first, last_in,
    z_s, z_r, c_s, c_r, y1_s, y1_r, y2_s, y2_r, x_s, x_r, gx_s, gx_r, g1_s, g1_r, g2_s, g2_r, gc_s, gc_r, k_s, k_r, f_s, f_r,
):
    dp, fs = lax.axis_index("dp"), lax.axis_index("fsdp")
    y, xh, core = dp // 4, (dp // 2) % 2, dp % 2
    xl, z = fs // 8, fs % 8

    def at(y, xh, core, xl, z):
        return (y * 4 + xh * 2 + core, xl * 8 + z)

    sibling = at(y, xh, 1 - core, xl, z)
    y_up, y_down = at((y + 1) % 4, xh, core, xl, z), at((y + 3) % 4, xh, core, xl, z)
    across = at(y, 1 - xh, core, xl, z)
    mate = at(y, xh, core, 1 - xl, z)
    z_up, z_down = at(y, xh, core, xl, (z + 1) % 8), at(y, xh, core, xl, (z + 7) % 8)

    def copy(src, dst, send, recv, device):
        return pltpu.make_async_remote_copy(
            src_ref=src, dst_ref=dst, send_sem=send, recv_sem=recv, device_id=device, device_id_type=MESH
        )

    def rows(start, size):
        return pl.ds(pl.multiple_of(start, ROW), size)

    def mine(quarter, half, size):
        return rows(core * BLOCK + ((y + quarter) % 4) * 32 + half * ROW, size)

    def z_copy(src, unit, side, device):
        return copy(src, toks.at[unit, rows(side * BLOCK, BLOCK)], z_s.at[unit, side], z_r.at[unit, side], device)

    def core_copy(i):
        return copy(part.at[i, rows((1 - core) * BLOCK, BLOCK)], core_in.at[i], c_s.at[i], c_r.at[i], sibling)

    def y_raw_copy(i, kind, quarter, half, device):
        return copy(part.at[i, mine(quarter, half, ROW)], y_raw.at[i, kind], y1_s.at[i, kind], y1_r.at[i, kind], device)

    def y_sum_copy(i, side, device):
        return copy(y_raw.at[i, side], y_sum.at[i, side], y2_s.at[i, side], y2_r.at[i, side], device)

    def pair_copy(i):
        return copy(pair.at[i, 1 - xh], pair_in.at[i], x_s.at[i], x_r.at[i], across)

    def acts_copy(i, where, send, recv, device):
        return copy(acts.at[i, where], acts.at[i, where], send, recv, device)

    def chain_copy(src, hr, way, step, device):
        return copy(src, chain_in.at[hr, way, step], k_s.at[hr, way, step], k_r.at[hr, way, step], device)

    def last_copy():
        return copy(outs.at[7, rows(0, BLOCK)], last_in, f_s.at[0], f_r.at[0], mate)

    def stage_xl(i):
        z_copy(own, 7, 0, mate).wait_recv()
        source = toks.at[7, rows(0, BLOCK)]
        z_copy(source, 4, 1, z_up).start()
        z_copy(source, 4, 0, z_down).start()

    def stage_z(i):
        p, hr = i % 4, i // 4
        low, high = toks.at[i, rows(BLOCK, BLOCK)], toks.at[i, rows(0, BLOCK)]
        z_copy(own, i, 1, z_up).wait_recv()

        @pl.when(p * 4 + hr * 2 < 10)
        def _():
            z_copy(low, i + 1, 1, z_up).start()

        @pl.when(p < 3)
        def _():
            z_copy(own, i, 0, z_down).wait_recv()

            @pl.when(p < 2)
            def _():
                z_copy(high, i + 1, 0, z_down).start()

            @pl.when(p + hr == 3)
            def _():
                z_copy(high, i + 1, 1, z_down).start()

    def stage_m(i):
        def one(k, carry):
            left = toks[i, :, pl.ds(pl.multiple_of(k // 2 * (FULL - 128), 128), FULL)]
            part[i, :, pl.ds(pl.multiple_of(k * HIDE, 128), HIDE)] = dot(left, w_in[k]).astype(BF16)
            return carry

        lax.fori_loop(0, 3, one, 0)
        core_copy(i).start()

    def stage_c(i):
        core_copy(i).wait_recv()

        def add(k, carry):
            quarter = k % 4
            here = mine(quarter, 0, 32)
            there = rows(((y + quarter) % 4) * 32, 32)
            part[i, here] = (part[i, here].astype(F32) + core_in[i, there].astype(F32)).astype(BF16)
            return carry

        lax.fori_loop(1, 4, add, 0)
        y_raw_copy(i, 0, 2, 0, y_up).start()
        y_raw_copy(i, 1, 2, 1, y_down).start()
        y_raw_copy(i, 2, 1, 1, y_up).start()
        y_raw_copy(i, 3, 3, 0, y_down).start()
        lax.fori_loop(4, 5, add, 0)

    def stage_y1(i):
        y_raw_copy(i, 0, 2, 0, y_up).wait_recv()
        y_raw[i, 0] = (y_raw[i, 0].astype(F32) + part[i, mine(1, 0, ROW)].astype(F32)).astype(BF16)
        y_sum_copy(i, 0, y_up).start()
        y_raw_copy(i, 1, 2, 1, y_down).wait_recv()
        y_raw[i, 1] = (y_raw[i, 1].astype(F32) + part[i, mine(3, 1, ROW)].astype(F32)).astype(BF16)
        y_sum_copy(i, 1, y_down).start()

    def stage_y2(i):
        y_raw_copy(i, 2, 1, 1, y_up).wait_recv()
        y_raw_copy(i, 3, 3, 0, y_down).wait_recv()
        y_sum_copy(i, 0, y_up).wait_recv()
        y_sum_copy(i, 1, y_down).wait_recv()
        for half, raw in ((0, 3), (1, 2)):
            total = part[i, mine(0, half, ROW)].astype(F32) + y_raw[i, raw].astype(F32) + y_sum[i, half].astype(F32)
            pair[i, half] = total.astype(BF16)
        pair_copy(i).start()

    def stage_x(i):
        pair_copy(i).wait_recv()
        total = pair[i, xh].astype(F32) + pair_in[i].astype(F32)
        gate, up, d_hidden = total[:, :HIDE], total[:, HIDE : 2 * HIDE], total[:, 2 * HIDE :]
        sigmoid = jax.nn.sigmoid(gate)
        activated = gate * sigmoid
        here = mine(0, xh, ROW)
        acts[i, here, pl.ds(0, HIDE)] = (activated * up).astype(BF16)
        acts[i, here, pl.ds(HIDE, HIDE)] = (d_hidden * up * sigmoid * (1.0 + gate * (1.0 - sigmoid))).astype(BF16)
        acts[i, here, pl.ds(2 * HIDE, HIDE)] = (d_hidden * activated).astype(BF16)
        acts_copy(i, here, gx_s.at[i], gx_r.at[i], across).start()

    def stage_g1(i):
        acts_copy(i, mine(0, 1 - xh, ROW), gx_s.at[i], gx_r.at[i], across).wait_recv()
        here = mine(0, 0, 32)
        acts_copy(i, here, g1_s.at[i, 0], g1_r.at[i, 0], y_up).start()
        acts_copy(i, here, g1_s.at[i, 1], g1_r.at[i, 1], y_down).start()
        acts_copy(i, here, gc_s.at[i, 0], gc_r.at[i, 0], sibling).start()

    def stage_g2(i):
        acts_copy(i, mine(3, 0, 32), g1_s.at[i, 0], g1_r.at[i, 0], y_up).wait_recv()
        acts_copy(i, mine(3, 0, ROW), g2_s.at[i, 0], g2_r.at[i, 0], y_up).start()
        acts_copy(i, mine(1, 0, 32), g1_s.at[i, 1], g1_r.at[i, 1], y_down).wait_recv()
        acts_copy(i, mine(1, 1, ROW), g2_s.at[i, 1], g2_r.at[i, 1], y_down).start()
        acts_copy(i, mine(3, 0, 32), gc_s.at[i, 1], gc_r.at[i, 1], sibling).start()
        acts_copy(i, mine(1, 0, 32), gc_s.at[i, 2], gc_r.at[i, 2], sibling).start()

    def stage_g3(i):
        acts_copy(i, mine(2, 0, ROW), g2_s.at[i, 0], g2_r.at[i, 0], y_up).wait_recv()
        acts_copy(i, mine(2, 1, ROW), g2_s.at[i, 1], g2_r.at[i, 1], y_down).wait_recv()
        acts_copy(i, mine(2, 0, 32), gc_s.at[i, 3], gc_r.at[i, 3], sibling).start()

    def stage_g4(i):
        for k, quarter in enumerate((0, 3, 1, 2)):
            there = rows((1 - core) * BLOCK + ((y + quarter) % 4) * 32, 32)
            acts_copy(i, there, gc_s.at[i, k], gc_r.at[i, k], sibling).wait_recv()
        output = dot(acts[i, :, pl.ds(0, HIDE)], w_out[0])
        d_tokens = dot(acts[i, :, pl.ds(HIDE, HIDE)], w_out[1]) + dot(acts[i, :, pl.ds(2 * HIDE, HIDE)], w_out[2])
        outs[i, :, pl.ds(0, FULL - 128)] = output[:, : FULL - 128].astype(BF16)
        outs[i, :, pl.ds(FULL - 128, 128)] = (output[:, FULL - 128 :] + d_tokens[:, :128]).astype(BF16)
        outs[i, :, pl.ds(FULL, FULL - 128)] = d_tokens[:, 128:].astype(BF16)

    def stage_w(i):
        left = toks[i, :, pl.ds(0, FULL)].T[:WIDE]
        grad_gate[...] += dot(left, acts[i, :, pl.ds(HIDE, HIDE)])
        grad_up[...] += dot(left, acts[i, :, pl.ds(2 * HIDE, HIDE)])
        left = toks[i, :, pl.ds(FULL - 128, FULL)].T[EDGE:]
        grad_down_t[...] += dot(left, acts[i, :, pl.ds(0, HIDE)])

    def stage_k(i):
        p, hr = i % 4, i // 4
        step = 3 - p
        ahead, behind = outs.at[i, rows(0, BLOCK)], outs.at[i, rows(BLOCK, BLOCK)]

        @pl.when(p == 3)
        def _():
            @pl.when(hr == 0)
            def _():
                chain_copy(behind, 0, 0, 0, z_up).start()

            @pl.when(hr == 1)
            def _():
                chain_copy(behind, 1, 1, 0, z_down).start()

        @pl.when(p < 3)
        def _():
            for way, block, device in ((0, ahead, z_up), (1, behind, z_down)):
                @pl.when((step > 1) | (hr == way))
                def _():
                    chain_copy(block, hr, way, step - 1, device).wait_recv()
                    block[...] = (block[...].astype(F32) + chain_in[hr, way, step - 1].astype(F32)).astype(BF16)

                chain_copy(block, hr, way, step, device).start()

    def stage_ki(hr):
        i = hr * 4 + 3
        block = outs.at[i, rows(0, BLOCK)]
        chain_copy(block, hr, 0, 3, z_up).wait_recv()
        chain_copy(block, hr, 1, 3, z_down).wait_recv()
        total = block[...].astype(F32) + chain_in[hr, 0, 3].astype(F32) + chain_in[hr, 1, 3].astype(F32)
        block[...] = total.astype(BF16)

        @pl.when(hr == 0)
        def _():
            first[...] = total

        @pl.when(hr == 1)
        def _():
            last_copy().start()

    barrier = pltpu.get_barrier_semaphore()
    peers = (sibling, y_up, y_down, across, mate, z_up, z_down)
    for device in peers:
        pl.semaphore_signal(barrier, inc=1, device_id=device, device_id_type=MESH)
    own[...] = jnp.concatenate((tokens_t[...], cotangent_t[...]), axis=0).T
    pl.semaphore_wait(barrier, len(peers))

    z_copy(own, 0, 1, z_up).start()
    z_copy(own, 0, 0, z_down).start()
    z_copy(own, 7, 0, mate).start()
    toks[3, rows(0, BLOCK)] = own[...]

    zeros = jnp.zeros((EDGE, HIDE), BF16)
    w_gate = (gate_codes[...].astype(F32) * gate_scale[...].reshape(1, HIDE)).astype(BF16)
    w_in[0, :WIDE] = w_gate
    w_in[0, WIDE:] = zeros
    w_out[1] = jnp.concatenate((zeros, w_gate), axis=0).T
    w_up = (up_codes[...].astype(F32) * up_scale[...].reshape(1, HIDE)).astype(BF16)
    w_in[1, :WIDE] = w_up
    w_in[1, WIDE:] = zeros
    w_out[2] = jnp.concatenate((zeros, w_up), axis=0).T
    w_down_t = (down_codes_t[...].astype(F32) * down_scale[...].reshape(WIDE, 1)).astype(BF16)
    w_in[2, :EDGE] = zeros
    w_in[2, EDGE:] = w_down_t
    w_out[0] = jnp.concatenate((w_down_t, zeros), axis=0).T
    grad_gate[...] = jnp.zeros_like(grad_gate)
    grad_up[...] = jnp.zeros_like(grad_up)
    grad_down_t[...] = jnp.zeros_like(grad_down_t)

    stages = (
        stage_xl, stage_z, stage_m, stage_c, stage_y1, stage_y2, stage_x, stage_g1, stage_g2, stage_g3, stage_g4,
        stage_w, stage_k, stage_ki,
    )

    codes = [KINDS.index(kind) * 8 + i for kind, i in ORDER]
    codes += [len(KINDS) * 8] * (-len(codes) % 4)
    words = [sum(code << (7 * k) for k, code in enumerate(codes[n : n + 4])) for n in range(0, len(codes), 4)]

    def step(k, word):
        kind, i = word // 8 % 16, word % 8
        for number, stage in enumerate(stages):
            pl.when(kind == number)(functools.partial(stage, i))
        return word // 128

    def four_steps(n, carry):
        word = jnp.int32(words[0])
        for k in range(1, len(words)):
            word = jnp.where(n == k, words[k], word)
        lax.fori_loop(0, 4, step, word)
        return carry

    lax.fori_loop(0, len(words), four_steps, 0)

    last_copy().wait_recv()
    total = (first[...] + last_in[...].astype(F32)).astype(BF16).T
    output_t[...] = total[:WIDE]
    d_tokens_t[...] = total[WIDE:]

    def sent(i, carry):
        p, hr = i % 4, i // 4
        z_copy(own, i, 1, z_up).wait_send()

        @pl.when(p < 3)
        def _():
            z_copy(own, i, 0, z_down).wait_send()

        core_copy(i).wait_send()
        for kind in range(4):
            y_raw_copy(i, kind, 0, 0, y_up).wait_send()
        for side in range(2):
            y_sum_copy(i, side, y_up).wait_send()
            acts_copy(i, mine(0, 0, 32), g1_s.at[i, side], g1_r.at[i, side], y_up).wait_send()
            acts_copy(i, mine(0, 0, ROW), g2_s.at[i, side], g2_r.at[i, side], y_up).wait_send()
        pair_copy(i).wait_send()
        acts_copy(i, mine(0, 0, ROW), gx_s.at[i], gx_r.at[i], across).wait_send()
        for k in range(4):
            acts_copy(i, mine(0, 0, 32), gc_s.at[i, k], gc_r.at[i, k], sibling).wait_send()
        for way in range(2):
            @pl.when((p > 0) | (hr == way))
            def _():
                chain_copy(own, hr, way, p, z_up).wait_send()

        return carry

    lax.fori_loop(0, UNITS, sent, 0)
    z_copy(own, 7, 0, mate).wait_send()
    last_copy().wait_send()


def local(tokens, cotangent, gate_codes, gate_scale, up_codes, up_scale, down_codes, down_scale):
    vmem = pl.BlockSpec(memory_space=pltpu.VMEM)
    dma = pltpu.SemaphoreType.DMA
    both = lambda *shape: [dma(shape), dma(shape)]
    output_t, d_tokens_t, grad_gate, grad_up, grad_down_t = pl.pallas_call(
        kernel,
        out_shape=(
            jax.ShapeDtypeStruct((WIDE, BLOCK), BF16),
            jax.ShapeDtypeStruct((WIDE, BLOCK), BF16),
            jax.ShapeDtypeStruct((WIDE, HIDE), F32),
            jax.ShapeDtypeStruct((WIDE, HIDE), F32),
            jax.ShapeDtypeStruct((WIDE, HIDE), F32),
        ),
        in_specs=[vmem] * 8,
        out_specs=(vmem,) * 5,
        scratch_shapes=[
            pltpu.VMEM((BLOCK, 2 * WIDE), BF16),
            pltpu.VMEM((UNITS, UNIT, 2 * WIDE), BF16),
            pltpu.VMEM((3, FULL, HIDE), BF16),
            pltpu.VMEM((3, HIDE, FULL), BF16),
            pltpu.VMEM((UNITS, UNIT, C), BF16),
            pltpu.VMEM((UNITS, BLOCK, C), BF16),
            pltpu.VMEM((UNITS, 4, ROW, C), BF16),
            pltpu.VMEM((UNITS, 2, ROW, C), BF16),
            pltpu.VMEM((UNITS, 2, ROW, C), BF16),
            pltpu.VMEM((UNITS, ROW, C), BF16),
            pltpu.VMEM((UNITS, UNIT, C), BF16),
            pltpu.VMEM((UNITS, UNIT, 2 * WIDE), BF16),
            pltpu.VMEM((2, 2, 4, BLOCK, 2 * WIDE), BF16),
            pltpu.VMEM((BLOCK, 2 * WIDE), F32),
            pltpu.VMEM((BLOCK, 2 * WIDE), BF16),
            *both(UNITS, 2),
            *both(UNITS),
            *both(UNITS, 4),
            *both(UNITS, 2),
            *both(UNITS),
            *both(UNITS),
            *both(UNITS, 2),
            *both(UNITS, 2),
            *both(UNITS, 4),
            *both(2, 2, 4),
            *both(1),
        ],
        compiler_params=pltpu.CompilerParams(
            collective_id=0, has_side_effects=True, vmem_limit_bytes=64 * 1024 * 1024 - 256 * 1024
        ),
    )(
        tokens.T, cotangent.T, gate_codes, gate_scale, up_codes, up_scale, down_codes.T, down_scale.reshape(WIDE)
    )
    return output_t.T, d_tokens_t.T, grad_gate, grad_up, grad_down_t.T


def solution(mesh):
    placed = (
        P("fsdp", "dp"),
        P("fsdp", "dp"),
        P("dp", "fsdp"),
        P("fsdp"),
        P("dp", "fsdp"),
        P("fsdp"),
        P("fsdp", "dp"),
        P(None, "dp"),
    )
    return jax.shard_map(
        local,
        mesh=mesh,
        in_specs=placed,
        out_specs=(
            P("fsdp", "dp"),
            P("fsdp", "dp"),
            P("dp", "fsdp"),
            P("dp", "fsdp"),
            P("fsdp", "dp"),
        ),
        check_vma=False,
    )
```

time: 647 us -> 149 us (0.23); the launches traced: 635 us -> 149 us
  waiting for transfers between devices: 552 us -> 0 us
  Pallas kernels: 0 us -> 139 us
  matrix products: 37.1 us -> 0 us
  local copies, waits for them, and re-layouts: 29.8 us -> 9.05 us
  between operations: 14.2 us -> 0.65 us
    unnamed x12 -> x0, waiting for transfers between devices: 297 us -> none
    all_gather x4 -> x0, waiting for transfers between devices: 255 us -> none  [the longest x1 71.1 us: local(): d_both_all = lax.all_gather(d_both, 'dp', axis=0, tiled=True)]
    pallas_call x0 -> x1, Pallas kernels: none -> 139 us  [local(): pl.pallas_call(kernel, out_shape=(jax.ShapeDtypeStruct((WIDE, BLOCK), BF1...]
    dot_general x6 -> x0, matrix products: 37.1 us -> none  [the longest x2 12.7 us: contract_rows(): lax.dot_general(left, right, (((0,), (0,)), ((), ())), preferred_element_...]
    unnamed x20 -> x9, local copies, waits for them, and re-layouts: 27.9 us -> 9.05 us
  transfers between devices with their start and end apart: 8 -> 0, of which waited for: 8 -> 0; matrix products, arithmetic and copies ran while one was open for 10% -> 0% of each run, Pallas kernels for 0% -> 0%
where the time goes in v1:
time: 149 us
  Pallas kernels  139 us (93%)
  local copies, waits for them, and re-layouts  9.05 us (6%)
    pallas_call x1, Pallas kernels, local(): pl.pallas_call(kernel, out_shape=(jax.ShapeDtypeStruct((WIDE, BLOCK), BF1...  139 us
    unnamed x9, local copies, waits for them, and re-layouts  9.05 us

profile of v1, /device:TPU:1, one launch (start us, length us, event | category | flops | bytes accessed | tf_op | source)
XLA Modules:
  0.0 148.9 jit_solution(1571748053057686452)
XLA Ops:
  0.6 139.2 %shard_map.119 = (bf16[448,128]{1,0:T(8,128)(2,1)}, bf16[448,128]{1,0:T(8,128)(2,1)}, f32[448,896]{1,0:T(8,128)}, f32[448,896]{1,0:T(8,128)}, f32[448,896]{1,0:T(8,128)}) custom-call(bf16[448,128]{1,0:T(8,128)(2,1)} %bitcast.11, bf16[448,128]{1,0:T(8,128)(2,1)} %bitcast.12, bf16[448,896]{1,0:T(8,128)(2,1)} %gate_codes.1, f32[896]{0:T(1024)} %gate_scale.1, ...), custom_call_target="tpu_custom_call" | custom-call | tf_op jit(solution)/shard_map/pallas_call | solution.py:352
  139.8 1.6 %copy.18 = bf16[128,448]{0,1:T(8,128)(2,1)} copy(bf16[128,448]{0,1:T(8,128)(2,1)} %bitcast.10) | data formatting | bytes 229376
  141.4 1.6 %copy.19 = bf16[128,448]{0,1:T(8,128)(2,1)} copy(bf16[128,448]{0,1:T(8,128)(2,1)} %bitcast.9) | data formatting | bytes 229376
  142.9 0.0 copy-start.1
  142.9 2.8 %copy.20 = f32[448,896]{1,0:T(8,128)} copy(f32[448,896]{1,0:T(8,128)} %get-tuple-element.22) | data formatting | bytes 3211264
  145.7 0.0 copy-done.1
  145.7 0.0 copy-start
  145.7 1.2 copy.21
  146.9 0.8 copy-done
  147.7 1.2 copy.22
Async XLA Ops:
  142.9 2.8 %copy-start.1 = (f32[448,896]{1,0:T(8,128)S(1)}, f32[448,896]{1,0:T(8,128)}, u32[]{:S(2)}) copy-start(f32[448,896]{1,0:T(8,128)} %get-tuple-element.23) | copy-start | bytes 4816900
  145.7 2.0 %copy-start = (f32[448,896]{1,0:T(8,128)S(1)}, f32[448,896]{1,0:T(8,128)}, u32[]{:S(2)}) copy-start(f32[448,896]{1,0:T(8,128)} %get-tuple-element.14) | copy-start | bytes 4816900

commit v2 on v1

v2 whole, which is shorter than its diff:
```python
import functools

import jax
import jax.numpy as jnp
from jax import lax
from jax.experimental import pallas as pl
from jax.experimental.pallas import tpu as pltpu
from jax.sharding import PartitionSpec as P

MESH = pl.DeviceIdType.MESH
BF16 = jnp.bfloat16
F32 = jnp.float32

BLOCK = 128
UNIT = 256
UNITS = 8
WIDE = 448
HIDE = 896
FULL = 512
C = 3 * HIDE
ROW = 16
HALF = 64
CUT = 11 * 128
EDGE = FULL - WIDE

ORDER = (
    ("Z", 0, 0), ("Z", 0, 1), ("M", 0, 0), ("Z", 1, 0), ("CX", 0, 0), ("Z", 1, 1), ("M", 1, 0), ("Z", 2, 0),
    ("C", 1, 0), ("Z", 2, 1), ("M", 2, 0), ("Z", 3, 0), ("XL", 0, 0), ("Y1", 1, 0), ("XL", 0, 1), ("C", 2, 0),
    ("Z", 3, 1), ("M", 3, 0), ("Z", 4, 0), ("Y2", 1, 0), ("Z", 7, 0), ("C", 3, 0), ("Y1", 2, 0), ("Z", 4, 1),
    ("M", 4, 0), ("Z", 7, 1), ("M", 7, 0), ("CX", 4, 0), ("Y1", 3, 0), ("Z", 5, 0), ("Z", 5, 1), ("C", 7, 0),
    ("M", 5, 0), ("C", 5, 0), ("Y2", 3, 0), ("Z", 6, 0), ("X", 1, 0), ("Y2", 2, 0), ("Z", 6, 1), ("Y1", 7, 0),
    ("Y1", 5, 0), ("M", 6, 0), ("XN", 3, 0), ("GA", 3, 0), ("Y2", 7, 0), ("C", 6, 0), ("X", 2, 0),
    ("G1X", 3, 0), ("Y1", 6, 0), ("XN", 7, 0), ("GA", 7, 0), ("G2X", 3, 0), ("G1", 2, 0), ("Y2", 6, 0),
    ("Y2", 5, 0), ("G1X", 7, 0), ("XA", 4, 0), ("G2", 2, 0), ("G3X", 3, 0), ("XN", 6, 0), ("G2X", 7, 0),
    ("GA", 6, 0), ("G4", 3, 0), ("K", 3, 0), ("Y1X", 4, 0), ("G3", 2, 0), ("G1", 1, 0), ("X", 5, 0),
    ("K", 3, 1), ("G1X", 6, 0), ("G4", 2, 0), ("K", 2, 0), ("G3X", 7, 0), ("G2", 1, 0), ("XX", 4, 0),
    ("XA", 0, 0), ("K", 2, 1), ("G4", 7, 0), ("SG", 3, 0), ("G1", 5, 0), ("K", 7, 0), ("G2X", 6, 0),
    ("K", 7, 1), ("G3", 1, 0), ("W", 2, 0), ("Y1X", 0, 0), ("G4", 1, 0), ("S", 2, 0), ("G2", 5, 0),
    ("K", 1, 0), ("G1", 4, 0), ("K", 1, 1), ("G3X", 6, 0), ("W", 1, 0), ("XX", 0, 0), ("G4", 6, 0),
    ("SG", 7, 0), ("K", 6, 0), ("K", 6, 1), ("G3", 5, 0), ("G2", 4, 0), ("W", 7, 0), ("G1", 0, 0),
    ("G4", 5, 0), ("S", 1, 0), ("K", 5, 0), ("G3", 4, 0), ("W", 3, 0), ("G2", 0, 0), ("K", 5, 1), ("G4", 4, 0),
    ("SG", 6, 0), ("K", 4, 0), ("G3", 0, 0), ("K", 4, 1), ("G4", 0, 0), ("S", 5, 0), ("K", 0, 0), ("KI", 1, 0),
    ("W", 5, 0), ("K", 0, 1), ("SX", 0, 0), ("SX", 4, 0), ("KI", 1, 1), ("W", 4, 0), ("W", 0, 0), ("KI", 0, 0),
    ("W", 6, 0), ("GO", 0, 0), ("KI", 0, 1),
)
KINDS = ("XL", "Z", "M", "C", "Y1", "Y2", "X", "G1", "G2", "G3", "G4", "W", "K", "KI", "S", "GO", "CX", "XA", "Y1X", "XX", "XN", "XXN", "GA", "G1X", "G2X", "G3X", "SX", "SG", "SXG")


def dot(left, right):
    return jnp.dot(left, right, preferred_element_type=F32)


def kernel(
    tokens_t, cotangent_t, gate_hbm, gate_scale, up_hbm, up_scale, down_hbm, down_scale,
    output_t, d_tokens_t, grads_hbm,
    codes, grads, load_sem, store_sem, own, toks, w_in, w_out, part, core_in, y_raw, y_sum, pair, pair_in, acts, outs, chain_in, first, last_in, side_in,
    z_s, z_r, c_s, c_r, y1_s, y1_r, y2_s, y2_r, x_s, x_r, gx_s, gx_r, g1_s, g1_r, g2_s, g2_r, gc_s, gc_r, k_s, k_r, f_s, f_r,
    a_s, a_r, b_s, b_r,
):
    dp, fs = lax.axis_index("dp"), lax.axis_index("fsdp")
    y, xh, core = dp // 4, (dp // 2) % 2, dp % 2
    xl, z = fs // 8, fs % 8

    def at(y, xh, core, xl, z):
        return (y * 4 + xh * 2 + core, xl * 8 + z)

    sibling = at(y, xh, 1 - core, xl, z)
    y_up, y_down = at((y + 1) % 4, xh, core, xl, z), at((y + 3) % 4, xh, core, xl, z)
    across = at(y, 1 - xh, core, xl, z)
    mate = at(y, xh, core, 1 - xl, z)
    z_up, z_down = at(y, xh, core, xl, (z + 1) % 8), at(y, xh, core, xl, (z + 7) % 8)

    def copy(src, dst, send, recv, device):
        return pltpu.make_async_remote_copy(
            src_ref=src, dst_ref=dst, send_sem=send, recv_sem=recv, device_id=device, device_id_type=MESH
        )

    def rows(start, size):
        return pl.ds(pl.multiple_of(start, ROW), size)

    def mine(quarter, half, size):
        return rows(core * BLOCK + ((y + quarter) % 4) * 32 + half * ROW, size)

    def z_copy(src, unit, side, half, device):
        dst = toks.at[unit, rows(side * BLOCK + half * HALF, HALF)]
        return copy(src, dst, z_s.at[unit, side, half], z_r.at[unit, side, half], device)

    def own_half(half):
        return own.at[rows(half * HALF, HALF)]

    def core_copy(i):
        return copy(part.at[i, rows((1 - core) * BLOCK, BLOCK)], core_in.at[i], c_s.at[i], c_r.at[i], sibling)

    def y_raw_copy(i, kind, quarter, half, device):
        return copy(part.at[i, mine(quarter, half, ROW)], y_raw.at[i, kind], y1_s.at[i, kind], y1_r.at[i, kind], device)

    def y_sum_copy(i, side, device):
        return copy(y_raw.at[i, side], y_sum.at[i, side], y2_s.at[i, side], y2_r.at[i, side], device)

    def pair_copy(i):
        return copy(pair.at[i, 1 - xh], pair_in.at[i], x_s.at[i], x_r.at[i], across)

    def acts_copy(i, where, send, recv, device):
        return copy(acts.at[i, where], acts.at[i, where], send, recv, device)

    def chain_copy(src, hr, way, step, half, device):
        where = (hr, way, step, half)
        return copy(src, chain_in.at[where], k_s.at[where], k_r.at[where], device)

    def last_copy(half):
        return copy(outs.at[7, rows(half * HALF, HALF)], last_in.at[half], f_s.at[half], f_r.at[half], mate)

    def stage_xl(i, half):
        z_copy(own_half(0), 7, 0, half, mate).wait_recv()
        source = toks.at[7, rows(half * HALF, HALF)]
        z_copy(source, 4, 1, half, z_up).start()
        z_copy(source, 4, 0, half, z_down).start()

    def stage_z(i, half):
        p, hr = i % 4, i // 4
        low = toks.at[i, rows(BLOCK + half * HALF, HALF)]
        high = toks.at[i, rows(half * HALF, HALF)]
        z_copy(own_half(0), i, 1, half, z_up).wait_recv()

        @pl.when(p * 4 + hr * 2 < 10)
        def _():
            z_copy(low, i + 1, 1, half, z_up).start()

        @pl.when(p < 3)
        def _():
            z_copy(own_half(0), i, 0, half, z_down).wait_recv()

            @pl.when(p < 2)
            def _():
                z_copy(high, i + 1, 0, half, z_down).start()

        @pl.when(i == 3)
        def _():
            z_copy(low, 7, 1, half, mate).start()

    def stage_m(i, half):
        for k, start in enumerate((0, 0, FULL - 128)):
            part[i, :, pl.ds(k * HIDE, HIDE)] = dot(toks[i, :, pl.ds(start, FULL)], w_in[k]).astype(BF16)
        core_copy(i).start()

    def stage_c(i, half):
        core_copy(i).wait_recv()

        def add(k, carry):
            quarter = k % 4
            here = mine(quarter, 0, 32)
            there = rows(((y + quarter) % 4) * 32, 32)
            part[i, here] = (part[i, here].astype(F32) + core_in[i, there].astype(F32)).astype(BF16)
            return carry

        lax.fori_loop(1, 4, add, 0)
        y_raw_copy(i, 0, 2, 0, y_up).start()
        y_raw_copy(i, 1, 2, 1, y_down).start()
        y_raw_copy(i, 2, 1, 1, y_up).start()
        y_raw_copy(i, 3, 3, 0, y_down).start()
        lax.fori_loop(4, 5, add, 0)

    def stage_y1(i, half):
        y_raw_copy(i, 0, 2, 0, y_up).wait_recv()
        y_raw[i, 0] = (y_raw[i, 0].astype(F32) + part[i, mine(1, 0, ROW)].astype(F32)).astype(BF16)
        y_sum_copy(i, 0, y_up).start()
        y_raw_copy(i, 1, 2, 1, y_down).wait_recv()
        y_raw[i, 1] = (y_raw[i, 1].astype(F32) + part[i, mine(3, 1, ROW)].astype(F32)).astype(BF16)
        y_sum_copy(i, 1, y_down).start()

    def stage_y2(i, half):
        y_raw_copy(i, 2, 1, 1, y_up).wait_recv()
        y_raw_copy(i, 3, 3, 0, y_down).wait_recv()
        y_sum_copy(i, 0, y_up).wait_recv()
        y_sum_copy(i, 1, y_down).wait_recv()
        for half, raw in ((0, 3), (1, 2)):
            total = part[i, mine(0, half, ROW)].astype(F32) + y_raw[i, raw].astype(F32) + y_sum[i, half].astype(F32)
            pair[i, half] = total.astype(BF16)
        pair_copy(i).start()

    def activate(i, total):
        gate, up, d_hidden = total[:, :HIDE], total[:, HIDE : 2 * HIDE], total[:, 2 * HIDE :]
        sigmoid = jax.nn.sigmoid(gate)
        activated = gate * sigmoid
        here = mine(0, xh, ROW)
        acts[i, here, pl.ds(0, HIDE)] = (activated * up).astype(BF16)
        acts[i, here, pl.ds(HIDE, HIDE)] = (d_hidden * up * sigmoid * (1.0 + gate * (1.0 - sigmoid))).astype(BF16)
        acts[i, here, pl.ds(2 * HIDE, HIDE)] = (d_hidden * activated).astype(BF16)

    def stage_xn(i, half):
        pair_copy(i).wait_recv()
        activate(i, pair[i, xh].astype(F32) + pair_in[i].astype(F32))

    def stage_x(i, half):
        stage_xn(i, half)
        acts_copy(i, mine(0, xh, ROW), gx_s.at[i], gx_r.at[i], across).start()

    cols = (pl.ds(0, CUT), pl.ds(CUT, C - CUT))

    def side_copy(i, k):
        return copy(part.at[i, mine(k, 1 - xh, ROW)], side_in.at[i, k], a_s.at[i, k], a_r.at[i, k], across)

    def raw_cols(i, kind, quarter, cut, device):
        where = cols[cut]
        source = part.at[i, mine(quarter, xh, ROW), where]
        return copy(source, y_raw.at[i, kind, :, where], y1_s.at[i, kind], y1_r.at[i, kind], device)

    def sum_cols(i, cut, device):
        where = cols[cut]
        return copy(y_raw.at[i, cut, :, where], y_sum.at[i, cut, :, where], y2_s.at[i, cut], y2_r.at[i, cut], device)

    def stage_cx(i, half):
        core_copy(i).wait_recv()

        def add(k, carry):
            here = mine(k, 0, 32)
            there = rows(((y + k) % 4) * 32, 32)
            part[i, here] = (part[i, here].astype(F32) + core_in[i, there].astype(F32)).astype(BF16)
            side_copy(i, k % 4).start()
            return carry

        lax.fori_loop(2, 6, add, 0)

    def stage_xa(i, half):
        for k in (2, 3, 1, 0):
            side_copy(i, k).wait_recv()
            here = mine(k, xh, ROW)
            part[i, here] = (part[i, here].astype(F32) + side_in[i, k].astype(F32)).astype(BF16)
            if k == 2:
                raw_cols(i, 0, 2, 0, y_up).start()
                raw_cols(i, 1, 2, 1, y_down).start()
            if k == 3:
                raw_cols(i, 3, 3, 0, y_down).start()
            if k == 1:
                raw_cols(i, 2, 1, 1, y_up).start()

    def stage_y1x(i, half):
        for cut, quarter, device in ((0, 1, y_up), (1, 3, y_down)):
            raw_cols(i, cut, 2, cut, device).wait_recv()
            where = cols[cut]
            term = part[i, mine(quarter, xh, ROW), where].astype(F32)
            y_raw[i, cut, :, where] = (y_raw[i, cut, :, where].astype(F32) + term).astype(BF16)
            sum_cols(i, cut, device).start()

    def stage_xxn(i, half):
        raw_cols(i, 2, 1, 1, y_up).wait_recv()
        raw_cols(i, 3, 3, 0, y_down).wait_recv()
        terms = []
        for cut, raw, device in ((0, 3, y_up), (1, 2, y_down)):
            sum_cols(i, cut, device).wait_recv()
            where = cols[cut]
            terms.append(
                part[i, mine(0, xh, ROW), where].astype(F32)
                + y_raw[i, raw, :, where].astype(F32)
                + y_sum[i, cut, :, where].astype(F32)
            )
        activate(i, jnp.concatenate(terms, axis=1))

    def stage_xx(i, half):
        stage_xxn(i, half)
        acts_copy(i, mine(0, xh, ROW), gx_s.at[i], gx_r.at[i], across).start()

    def g1_cols(i, way, part_no, quarter, device):
        where = (i, mine(quarter, xh, ROW), cols[way ^ part_no])
        return copy(acts.at[where], acts.at[where], g1_s.at[i, way, part_no], g1_r.at[i, way, part_no], device)

    def g2_cols(i, way, quarter, device):
        where = (i, mine(quarter, xh, ROW), cols[way])
        return copy(acts.at[where], acts.at[where], g2_s.at[i, way], g2_r.at[i, way], device)

    def ga_copy(i, k, half):
        return acts_copy(i, mine((0, 3, 1, 2)[k], half, ROW), b_s.at[i, k], b_r.at[i, k], across)

    def stage_ga(i, half):
        for n in range(2):
            g1_cols(i, 0, n, 0, y_up).start()
            g1_cols(i, 1, n, 0, y_down).start()
        ga_copy(i, 0, xh).start()

    def stage_g1x(i, half):
        g1_cols(i, 0, 0, 3, y_up).wait_recv()
        g2_cols(i, 0, 3, y_up).start()
        g1_cols(i, 1, 0, 1, y_down).wait_recv()
        g2_cols(i, 1, 1, y_down).start()
        g1_cols(i, 0, 1, 3, y_up).wait_recv()
        ga_copy(i, 1, xh).start()
        g1_cols(i, 1, 1, 1, y_down).wait_recv()
        ga_copy(i, 2, xh).start()

    def stage_g2x(i, half):
        g2_cols(i, 0, 2, y_up).wait_recv()
        g2_cols(i, 1, 2, y_down).wait_recv()
        ga_copy(i, 3, xh).start()

    def stage_g3x(i, half):
        for k, quarter in enumerate((0, 3, 1, 2)):
            ga_copy(i, k, 1 - xh).wait_recv()
            acts_copy(i, mine(quarter, 0, 32), gc_s.at[i, k], gc_r.at[i, k], sibling).start()

    def g1_copy(i, way, part_no, where, device):
        return acts_copy(i, where, g1_s.at[i, way, part_no], g1_r.at[i, way, part_no], device)

    def stage_g1(i, half):
        acts_copy(i, mine(0, 1 - xh, ROW), gx_s.at[i], gx_r.at[i], across).wait_recv()
        g1_copy(i, 0, 0, mine(0, 0, ROW), y_up).start()
        g1_copy(i, 1, 0, mine(0, 1, ROW), y_down).start()
        g1_copy(i, 0, 1, mine(0, 1, ROW), y_up).start()
        g1_copy(i, 1, 1, mine(0, 0, ROW), y_down).start()
        acts_copy(i, mine(0, 0, 32), gc_s.at[i, 0], gc_r.at[i, 0], sibling).start()

    def stage_g2(i, half):
        g1_copy(i, 0, 0, mine(3, 0, ROW), y_up).wait_recv()
        acts_copy(i, mine(3, 0, ROW), g2_s.at[i, 0], g2_r.at[i, 0], y_up).start()
        g1_copy(i, 1, 0, mine(1, 1, ROW), y_down).wait_recv()
        acts_copy(i, mine(1, 1, ROW), g2_s.at[i, 1], g2_r.at[i, 1], y_down).start()

    def stage_g3(i, half):
        g1_copy(i, 0, 1, mine(3, 1, ROW), y_up).wait_recv()
        acts_copy(i, mine(3, 0, 32), gc_s.at[i, 1], gc_r.at[i, 1], sibling).start()
        g1_copy(i, 1, 1, mine(1, 0, ROW), y_down).wait_recv()
        acts_copy(i, mine(1, 0, 32), gc_s.at[i, 2], gc_r.at[i, 2], sibling).start()
        acts_copy(i, mine(2, 0, ROW), g2_s.at[i, 0], g2_r.at[i, 0], y_up).wait_recv()
        acts_copy(i, mine(2, 1, ROW), g2_s.at[i, 1], g2_r.at[i, 1], y_down).wait_recv()
        acts_copy(i, mine(2, 0, 32), gc_s.at[i, 3], gc_r.at[i, 3], sibling).start()

    def stage_g4(i, half):
        for k, quarter in enumerate((0, 3, 1, 2)):
            there = rows((1 - core) * BLOCK + ((y + quarter) % 4) * 32, 32)
            acts_copy(i, there, gc_s.at[i, k], gc_r.at[i, k], sibling).wait_recv()
        output = dot(acts[i, :, pl.ds(0, HIDE)], w_out[0])
        d_tokens = dot(acts[i, :, pl.ds(HIDE, HIDE)], w_out[1]) + dot(acts[i, :, pl.ds(2 * HIDE, HIDE)], w_out[2])
        outs[i, :, pl.ds(0, FULL - 128)] = output[:, : FULL - 128].astype(BF16)
        outs[i, :, pl.ds(FULL - 128, 128)] = (output[:, FULL - 128 :] + d_tokens[:, :128]).astype(BF16)
        outs[i, :, pl.ds(FULL, FULL - 128)] = d_tokens[:, 128:].astype(BF16)

    def stage_w(i, half):
        left = toks[i, :, pl.ds(0, FULL)].T[:WIDE]
        grads[0] += dot(left, acts[i, :, pl.ds(HIDE, HIDE)])
        grads[1] += dot(left, acts[i, :, pl.ds(2 * HIDE, HIDE)])
        left = toks[i, :, pl.ds(FULL - 128, FULL)].T[EDGE:]
        grads[2] += dot(left, acts[i, :, pl.ds(0, HIDE)])

    def stage_k(i, half):
        p, hr = i % 4, i // 4
        step = 3 - p
        ahead, behind = outs.at[i, rows(half * HALF, HALF)], outs.at[i, rows(BLOCK + half * HALF, HALF)]

        @pl.when(p == 3)
        def _():
            @pl.when(hr == 0)
            def _():
                chain_copy(behind, 0, 0, 0, half, z_up).start()

            @pl.when(hr == 1)
            def _():
                chain_copy(behind, 1, 1, 0, half, z_down).start()

        @pl.when(p < 3)
        def _():
            for way, block, device in ((0, ahead, z_up), (1, behind, z_down)):
                @pl.when((step > 1) | (hr == way))
                def _():
                    chain_copy(block, hr, way, step - 1, half, device).wait_recv()
                    block[...] = (block[...].astype(F32) + chain_in[hr, way, step - 1, half].astype(F32)).astype(BF16)

                chain_copy(block, hr, way, step, half, device).start()

    def stage_ki(hr, half):
        here = rows(half * HALF, HALF)
        block = outs.at[hr * 4 + 3, here]
        chain_copy(block, hr, 0, 3, half, z_up).wait_recv()
        chain_copy(block, hr, 1, 3, half, z_down).wait_recv()
        total = block[...].astype(F32) + chain_in[hr, 0, 3, half].astype(F32) + chain_in[hr, 1, 3, half].astype(F32)
        block[...] = total.astype(BF16)

        @pl.when(hr == 0)
        def _():
            first[here] = total

        @pl.when(hr == 1)
        def _():
            last_copy(half).start()

    def sends_of(by_side, by_ring):
        def stage(i, half):
            p = i % 4
            for n in range(2):
                z_copy(own_half(0), i, 1, n, z_up).wait_send()

                @pl.when(p < 3)
                def _():
                    z_copy(own_half(0), i, 0, n, z_down).wait_send()

            core_copy(i).wait_send()
            for way in range(2):
                if by_side:
                    raw_cols(i, way, 2, way, y_up).wait_send()
                    raw_cols(i, 3 - way, 2, way, y_up).wait_send()
                    sum_cols(i, way, y_up).wait_send()
                else:
                    y_raw_copy(i, way, 0, 0, y_up).wait_send()
                    y_raw_copy(i, 3 - way, 0, 0, y_up).wait_send()
                    y_sum_copy(i, way, y_up).wait_send()
                for n in range(2):
                    if by_ring:
                        g1_cols(i, way, n, 0, y_up).wait_send()
                    else:
                        g1_copy(i, way, n, mine(0, 0, ROW), y_up).wait_send()
                if by_ring:
                    g2_cols(i, way, 0, y_up).wait_send()
                else:
                    acts_copy(i, mine(0, 0, ROW), g2_s.at[i, way], g2_r.at[i, way], y_up).wait_send()
            if by_side:
                for k in range(4):
                    side_copy(i, k).wait_send()
            else:
                pair_copy(i).wait_send()
            if by_ring:
                for k in range(4):
                    ga_copy(i, k, xh).wait_send()
            else:
                acts_copy(i, mine(0, 0, ROW), gx_s.at[i], gx_r.at[i], across).wait_send()
            for k in range(4):
                acts_copy(i, mine(0, 0, 32), gc_s.at[i, k], gc_r.at[i, k], sibling).wait_send()

        return stage

    def store(k):
        return pltpu.make_async_copy(grads.at[k], grads_hbm.at[k], store_sem.at[k])

    def stage_go(i, half):
        @pl.when(i == 0)
        def _():
            for k in range(3):
                store(k).start()

    loads = [
        pltpu.make_async_copy(ref, codes.at[k], load_sem.at[k]) for k, ref in enumerate((gate_hbm, up_hbm, down_hbm))
    ]
    for load in loads:
        load.start()
    barrier = pltpu.get_barrier_semaphore()
    peers = (sibling, y_up, y_down, across, mate, z_up, z_down)
    for device in peers:
        pl.semaphore_signal(barrier, inc=1, device_id=device, device_id_type=MESH)
    own[...] = jnp.concatenate((tokens_t[...], cotangent_t[...]), axis=0).T
    pl.semaphore_wait(barrier, len(peers))

    for half in range(2):
        z_copy(own_half(half), 0, 1, half, z_up).start()
        z_copy(own_half(half), 0, 0, half, z_down).start()
        z_copy(own_half(half), 7, 0, half, mate).start()
    toks[3, rows(0, BLOCK)] = own[...]

    zeros = jnp.zeros((EDGE, HIDE), BF16)
    grads[...] = jnp.zeros_like(grads)
    loads[0].wait()
    w_gate = (codes[0].astype(F32) * gate_scale[...].reshape(1, HIDE)).astype(BF16)
    w_in[0, :WIDE] = w_gate
    w_in[0, WIDE:] = zeros
    w_out[1] = jnp.concatenate((zeros, w_gate), axis=0).T
    loads[1].wait()
    w_up = (codes[1].astype(F32) * up_scale[...].reshape(1, HIDE)).astype(BF16)
    w_in[1, :WIDE] = w_up
    w_in[1, WIDE:] = zeros
    w_out[2] = jnp.concatenate((zeros, w_up), axis=0).T
    loads[2].wait()
    w_down_t = (codes[2].astype(F32) * down_scale[...].reshape(WIDE, 1)).astype(BF16)
    w_in[2, :EDGE] = zeros
    w_in[2, EDGE:] = w_down_t
    w_out[0] = jnp.concatenate((w_down_t, zeros), axis=0).T

    stages = (
        stage_xl, stage_z, stage_m, stage_c, stage_y1, stage_y2, stage_x, stage_g1, stage_g2, stage_g3, stage_g4,
        stage_w, stage_k, stage_ki, sends_of(False, False), stage_go, stage_cx, stage_xa, stage_y1x, stage_xx, stage_xn,
        stage_xxn, stage_ga, stage_g1x, stage_g2x, stage_g3x, sends_of(True, False), sends_of(False, True),
        sends_of(True, True),
    )

    steps = [KINDS.index(kind) * 16 + half * 8 + i for kind, i, half in ORDER]
    steps += [KINDS.index("GO") * 16 + 1] * (-len(steps) % 3)
    words = [sum(code << (9 * k) for k, code in enumerate(steps[n : n + 3])) for n in range(0, len(steps), 3)]
    groups = [stages[n : n + 4] for n in range(0, len(stages), 4)]

    def step(k, word):
        kind, half, i = word // 16 % 32, word // 8 % 2, word % 8
        for n, group in enumerate(groups):
            @pl.when(kind // 4 == n)
            def _():
                for number, stage in enumerate(group):
                    pl.when(kind % 4 == number)(functools.partial(stage, i, half))

        return word // 512

    def three_steps(n, carry):
        word = jnp.int32(words[0])
        for k in range(1, len(words)):
            word = jnp.where(n == k, words[k], word)
        lax.fori_loop(0, 3, step, word)
        return carry

    lax.fori_loop(0, len(words), three_steps, 0)

    for half in range(2):
        last_copy(half).wait_recv()
    total = (first[...] + last_in[...].reshape(BLOCK, 2 * WIDE).astype(F32)).astype(BF16).T
    output_t[...] = total[:WIDE]
    d_tokens_t[...] = total[WIDE:]

    for hr in range(2):
        for way in range(2):
            for n in range(4):
                for half in range(2):
                    if n > 0 or hr == way:
                        chain_copy(own_half(0), hr, way, n, half, z_up).wait_send()
    for half in range(2):
        z_copy(own_half(0), 7, 0, half, mate).wait_send()
        last_copy(half).wait_send()
    for k in range(3):
        store(k).wait()


def settle(*refs):
    ins, outs, held, sems = refs[:3], refs[3:8], refs[8:13], refs[13:]
    sources = [*ins[:2], *(ins[2].at[k] for k in range(3))]
    loads = [pltpu.make_async_copy(a, b, sems[0].at[k]) for k, (a, b) in enumerate(zip(sources, held))]
    stores = [pltpu.make_async_copy(a, b, sems[1].at[k]) for k, (a, b) in enumerate(zip(held, outs))]
    for one in loads:
        one.start()
    for load, one in zip(loads, stores):
        load.wait()
        one.start()
    for one in stores:
        one.wait()


def local(tokens, cotangent, gate_codes, gate_scale, up_codes, up_scale, down_codes, down_scale):
    vmem = pl.BlockSpec(memory_space=pltpu.VMEM)
    dma = pltpu.SemaphoreType.DMA
    both = lambda *shape: [dma(shape), dma(shape)]
    anywhere = pl.BlockSpec(memory_space=pl.ANY)
    edge = jax.ShapeDtypeStruct((WIDE, BLOCK), BF16)
    results = pl.pallas_call(
        kernel,
        out_shape=(edge, edge, jax.ShapeDtypeStruct((3, WIDE, HIDE), F32)),
        in_specs=[vmem, vmem, anywhere, vmem, anywhere, vmem, anywhere, vmem],
        out_specs=(vmem, vmem, anywhere),
        scratch_shapes=[
            pltpu.VMEM((3, WIDE, HIDE), BF16),
            pltpu.VMEM((3, WIDE, HIDE), F32),
            dma((3,)),
            dma((3,)),
            pltpu.VMEM((BLOCK, 2 * WIDE), BF16),
            pltpu.VMEM((UNITS, UNIT, 2 * WIDE), BF16),
            pltpu.VMEM((3, FULL, HIDE), BF16),
            pltpu.VMEM((3, HIDE, FULL), BF16),
            pltpu.VMEM((UNITS, UNIT, C), BF16),
            pltpu.VMEM((UNITS, BLOCK, C), BF16),
            pltpu.VMEM((UNITS, 4, ROW, C), BF16),
            pltpu.VMEM((UNITS, 2, ROW, C), BF16),
            pltpu.VMEM((UNITS, 2, ROW, C), BF16),
            pltpu.VMEM((UNITS, ROW, C), BF16),
            pltpu.VMEM((UNITS, UNIT, C), BF16),
            pltpu.VMEM((UNITS, UNIT, 2 * WIDE), BF16),
            pltpu.VMEM((2, 2, 4, 2, HALF, 2 * WIDE), BF16),
            pltpu.VMEM((BLOCK, 2 * WIDE), F32),
            pltpu.VMEM((2, HALF, 2 * WIDE), BF16),
            pltpu.VMEM((UNITS, 4, ROW, C), BF16),
            *both(UNITS, 2, 2),
            *both(UNITS),
            *both(UNITS, 4),
            *both(UNITS, 2),
            *both(UNITS),
            *both(UNITS),
            *both(UNITS, 2, 2),
            *both(UNITS, 2),
            *both(UNITS, 4),
            *both(2, 2, 4, 2),
            *both(2),
            *both(UNITS, 4),
            *both(UNITS, 4),
        ],
        compiler_params=pltpu.CompilerParams(
            collective_id=0, has_side_effects=True, vmem_limit_bytes=64 * 1024 * 1024 - 256 * 1024
        ),
    )(
        tokens.T, cotangent.T, gate_codes, gate_scale, up_codes, up_scale, down_codes.T, down_scale.reshape(WIDE)
    )
    grad = jax.ShapeDtypeStruct((WIDE, HIDE), F32)
    output_t, d_tokens_t, grad_gate, grad_up, grad_down_t = pl.pallas_call(
        settle,
        out_shape=(edge, edge, grad, grad, grad),
        in_specs=[anywhere] * 3,
        out_specs=(anywhere,) * 5,
        scratch_shapes=[pltpu.VMEM((WIDE, BLOCK), BF16)] * 2 + [pltpu.VMEM((WIDE, HIDE), F32)] * 3 + [dma((5,))] * 2,
        compiler_params=pltpu.CompilerParams(vmem_limit_bytes=60 * 1024 * 1024),
    )(*results)
    return output_t.T, d_tokens_t.T, grad_gate, grad_up, grad_down_t.T


def solution(mesh):
    placed = (
        P("fsdp", "dp"),
        P("fsdp", "dp"),
        P("dp", "fsdp"),
        P("fsdp"),
        P("dp", "fsdp"),
        P("fsdp"),
        P("fsdp", "dp"),
        P(None, "dp"),
    )
    return jax.shard_map(
        local,
        mesh=mesh,
        in_specs=placed,
        out_specs=(
            P("fsdp", "dp"),
            P("fsdp", "dp"),
            P("dp", "fsdp"),
            P("dp", "fsdp"),
            P("fsdp", "dp"),
        ),
        check_vma=False,
    )
```

time: 149 us -> 128 us (0.86)
  Pallas kernels: 139 us -> 128 us
  local copies, waits for them, and re-layouts: 9.05 us -> 0 us
    pallas_call x1 -> x2, Pallas kernels: 139 us -> 128 us  [the longest x1 124 us: local(): pl.pallas_call(kernel, out_shape=(edge, edge, jax.ShapeDtypeStruct((3, WI...]
    unnamed x9 -> x0, local copies, waits for them, and re-layouts: 9.05 us -> none
where the time goes in v2:
time: 128 us
  Pallas kernels  128 us (100%)
    pallas_call x1, Pallas kernels, local(): pl.pallas_call(kernel, out_shape=(edge, edge, jax.ShapeDtypeStruct((3, WI...  124 us
    pallas_call x1, Pallas kernels, local(): pl.pallas_call(settle, out_shape=(edge, edge, grad, grad, grad), in_specs...  4.01 us

profile of v2, /device:TPU:1, one launch (start us, length us, event | category | flops | bytes accessed | tf_op | source)
XLA Modules:
  0.0 128.2 jit_solution(12902652025797038555)
XLA Ops:
  0.6 123.5 %shard_map.119 = (bf16[448,128]{1,0:T(8,128)(2,1)}, bf16[448,128]{1,0:T(8,128)(2,1)}, f32[3,448,896]{2,1,0:T(8,128)}) custom-call(bf16[448,128]{1,0:T(8,128)(2,1)} %bitcast.8, bf16[448,128]{1,0:T(8,128)(2,1)} %bitcast.9, bf16[448,896]{1,0:T(8,128)(2,1)} %gate_hbm.1, f32[896]{0:T(1024)} %gate_scale.1, bf16[448,896]{1,0:T(8,128)(2,1)} %up_hbm.1, ...), custom_call_target="tpu_custom_call" | custom-call | tf_op jit(solution)/shard_map/pallas_call | solution.py:543
  124.2 4.0 %shard_map.120 = (bf16[448,128]{1,0:T(8,128)(2,1)}, bf16[448,128]{1,0:T(8,128)(2,1)}, f32[448,896]{1,0:T(8,128)}, f32[448,896]{1,0:T(8,128)}, f32[448,896]{1,0:T(8,128)}) custom-call(bf16[448,128]{1,0:T(8,128)(2,1)} %get-tuple-element.13.refs_0_, bf16[448,128]{1,0:T(8,128)(2,1)} %get-tuple-element.14.refs_1_, f32[3,448,896]{2,1,0:T(8,128)} %get-tuple-element.15.refs_2_), custom_call_target="tpu_custom_call" | custom-call | tf_op jit(solution)/shard_map/pallas_call | solution.py:590

commit v3 on v2

v3 whole, which is shorter than its diff:
```python
import functools

import jax
import jax.numpy as jnp
from jax import lax
from jax.experimental import pallas as pl
from jax.experimental.pallas import tpu as pltpu
from jax.sharding import PartitionSpec as P

MESH = pl.DeviceIdType.MESH
BF16 = jnp.bfloat16
F32 = jnp.float32

BLOCK = 128
UNIT = 256
UNITS = 8
WIDE = 448
HIDE = 896
FULL = 512
C = 3 * HIDE
ROW = 16
Z_PARTS = 4
Z_ROWS = BLOCK // Z_PARTS
CHAIN_PARTS = 2
CHAIN_ROWS = BLOCK // CHAIN_PARTS
CUT = 11 * 128
EDGE = FULL - WIDE

ORDER = (
    ("Z", 0, 0), ("Z", 0, 1), ("Z", 0, 2), ("Z", 0, 3), ("M", 0, 0), ("Z", 1, 0), ("Z", 1, 1), ("Z", 1, 2),
    ("CX", 0, 0), ("Z", 1, 3), ("M", 1, 0), ("Z", 2, 0), ("Z", 2, 1), ("Z", 2, 2), ("C", 1, 0), ("Z", 2, 3),
    ("XL", 0, 0), ("M", 2, 0), ("Z", 3, 0), ("Z", 3, 1), ("Y1", 1, 0), ("Z", 3, 2), ("XL", 0, 1), ("XL", 0, 2),
    ("C", 2, 0), ("Z", 3, 3), ("M", 3, 0), ("XL", 0, 3), ("Z", 4, 0), ("Z", 7, 0), ("Y2", 1, 0), ("Z", 4, 1),
    ("Z", 4, 2), ("C", 3, 0), ("Z", 7, 1), ("Z", 7, 2), ("Z", 4, 3), ("M", 4, 0), ("Z", 7, 3), ("XA", 0, 0),
    ("Z", 5, 0), ("M", 7, 0), ("Z", 5, 1), ("Y1", 3, 0), ("CX", 4, 0), ("Z", 5, 2), ("Z", 5, 3), ("Z", 6, 0),
    ("C", 7, 0), ("Z", 6, 1), ("Y1", 2, 0), ("Z", 6, 2), ("Z", 6, 3), ("M", 6, 0), ("Y2", 3, 0), ("Y1", 7, 0),
    ("C", 6, 0), ("Y2", 2, 0), ("Y2", 7, 0), ("XN", 3, 0), ("GA", 3, 0), ("M", 5, 0), ("Y1", 6, 0),
    ("X", 1, 0), ("G1X", 3, 0), ("X", 2, 0), ("C", 5, 0), ("XN", 7, 0), ("Y2", 6, 0), ("G2X", 3, 0),
    ("GA", 7, 0), ("Y1", 5, 0), ("G1X", 7, 0), ("G1", 2, 0), ("XN", 6, 0), ("Y2", 5, 0), ("G3X", 3, 0),
    ("G2X", 7, 0), ("G2", 2, 0), ("GA", 6, 0), ("G4", 3, 0), ("XA", 4, 0), ("K", 3, 0), ("K", 3, 1),
    ("G3", 2, 0), ("X", 5, 0), ("G1X", 6, 0), ("G1", 1, 0), ("G4", 2, 0), ("K", 2, 0), ("G2X", 6, 0),
    ("G3X", 7, 0), ("G2", 1, 0), ("K", 2, 1), ("Y1X", 4, 0), ("G4", 7, 0), ("Y1X", 0, 0), ("K", 7, 0),
    ("G1", 5, 0), ("G3", 1, 0), ("K", 7, 1), ("XX", 4, 0), ("W", 3, 0), ("G4", 1, 0), ("K", 1, 0),
    ("G2", 5, 0), ("G3X", 6, 0), ("XX", 0, 0), ("G1", 4, 0), ("K", 1, 1), ("G4", 6, 0), ("K", 6, 0),
    ("G3", 5, 0), ("G2", 4, 0), ("K", 6, 1), ("W", 1, 0), ("G1", 0, 0), ("G4", 5, 0), ("K", 5, 0),
    ("G3", 4, 0), ("W", 5, 0), ("G2", 0, 0), ("K", 5, 1), ("G4", 4, 0), ("K", 4, 0), ("G3", 0, 0), ("K", 4, 1),
    ("W", 7, 0), ("G4", 0, 0), ("KI", 1, 0), ("K", 0, 0), ("K", 0, 1), ("KI", 1, 1), ("W", 6, 0), ("W", 2, 0),
    ("W", 4, 0), ("W", 0, 0), ("GO", 0, 0), ("S", 7, 0), ("S", 6, 0), ("S", 5, 0), ("S", 4, 0), ("S", 3, 0),
    ("S", 2, 0), ("S", 1, 0), ("S", 0, 0), ("KI", 0, 0), ("KI", 0, 1),
)
KINDS = ("XL", "Z", "M", "C", "Y1", "Y2", "X", "G1", "G2", "G3", "G4", "W", "K", "KI", "S", "GO", "CX", "XA", "Y1X", "XX", "XN", "XXN", "GA", "G1X", "G2X", "G3X")


def dot(left, right):
    return jnp.dot(left, right, preferred_element_type=F32)


def kernel(
    tokens_hbm, cotangent_hbm, gate_hbm, gate_scale, up_hbm, up_scale, down_hbm, down_scale,
    output_t, d_tokens_t, grads_hbm,
    features_t, codes, grads, load_sem, store_sem, own, toks, w_in, w_out, part, core_in, y_raw, y_sum, pair, pair_in, acts, outs, chain_in, first, last_in, side_in,
    z_s, dp_s, k_s, f_s,
    z_r, xl_r, c_r, y1_r, y2_r, x_r, gx_r, g1_r, g2_r, gc_r, k_r, f_r,
):
    dp, fs = lax.axis_index("dp"), lax.axis_index("fsdp")
    y, xh, core = dp // 4, (dp // 2) % 2, dp % 2
    xl, z = fs // 8, fs % 8

    def at(y, xh, core, xl, z):
        return (y * 4 + xh * 2 + core, xl * 8 + z)

    sibling = at(y, xh, 1 - core, xl, z)
    y_up, y_down = at((y + 1) % 4, xh, core, xl, z), at((y + 3) % 4, xh, core, xl, z)
    across = at(y, 1 - xh, core, xl, z)
    mate = at(y, xh, core, 1 - xl, z)
    z_up, z_down = at(y, xh, core, xl, (z + 1) % 8), at(y, xh, core, xl, (z + 7) % 8)

    def copy(src, dst, send, recv, device):
        return pltpu.make_async_remote_copy(
            src_ref=src, dst_ref=dst, send_sem=send, recv_sem=recv, device_id=device, device_id_type=MESH
        )

    def rows(start, size):
        return pl.ds(pl.multiple_of(start, ROW), size)

    def mine(quarter, half, size):
        return rows(core * BLOCK + ((y + quarter) % 4) * 32 + half * ROW, size)

    def await_bytes(ref, semaphore):
        pltpu.make_async_copy(ref, ref, semaphore).wait()

    def wide_rows(count):
        return core_in.at[rows(0, count)]

    def z_copy(src, unit, side, half, device):
        dst = toks.at[unit, rows(side * BLOCK + half * Z_ROWS, Z_ROWS)]
        return copy(src, dst, z_s.at[unit], z_r.at[unit, half], device)

    def xl_copy(half):
        return copy(own_half(half), toks.at[7, rows(half * Z_ROWS, Z_ROWS)], z_s.at[7], xl_r.at[half], mate)

    def own_half(half):
        return own.at[rows(half * Z_ROWS, Z_ROWS)]

    def core_copy(i):
        source = part.at[i, rows((1 - core) * BLOCK, BLOCK)]
        return copy(source, core_in.at[rows(i * BLOCK, BLOCK)], dp_s.at[i], c_r.at[i], sibling)

    def y_raw_copy(i, kind, quarter, half, device):
        landed = (y1_r if kind < 2 else y2_r).at[i]
        return copy(part.at[i, mine(quarter, half, ROW)], y_raw.at[i, kind], dp_s.at[i], landed, device)

    def y_sum_copy(i, side, device):
        return copy(y_raw.at[i, side], y_sum.at[i, side], dp_s.at[i], y2_r.at[i], device)

    def pair_copy(i):
        return copy(pair.at[i, 1 - xh], pair_in.at[i], dp_s.at[i], x_r.at[i], across)

    def acts_copy(i, where, landed, device):
        return copy(acts.at[i, where], acts.at[i, where], dp_s.at[i], landed.at[i], device)

    def chain_copy(src, hr, way, step, half, device):
        return copy(src, chain_in.at[hr, way, step, half], k_s.at[0], k_r.at[hr, step, half], device)

    def last_copy(half):
        return copy(outs.at[7, rows(half * CHAIN_ROWS, CHAIN_ROWS)], last_in.at[half], f_s.at[0], f_r.at[0], mate)

    def stage_xl(i, half):
        xl_copy(half).wait_recv()
        source = toks.at[7, rows(half * Z_ROWS, Z_ROWS)]
        z_copy(source, 4, 1, half, z_up).start()
        z_copy(source, 4, 0, half, z_down).start()

    def stage_z(i, half):
        p, hr = i % 4, i // 4
        low = toks.at[i, rows(BLOCK + half * Z_ROWS, Z_ROWS)]
        high = toks.at[i, rows(half * Z_ROWS, Z_ROWS)]

        @pl.when(p < 3)
        def _():
            await_bytes(toks.at[i, rows(0, 2 * Z_ROWS)], z_r.at[i, half])

        @pl.when(p == 3)
        def _():
            await_bytes(toks.at[i, rows(BLOCK, Z_ROWS)], z_r.at[i, half])

        @pl.when(p * 4 + hr * 2 < 10)
        def _():
            z_copy(low, i + 1, 1, half, z_up).start()

        @pl.when(p < 2)
        def _():
            z_copy(high, i + 1, 0, half, z_down).start()

        @pl.when(i == 3)
        def _():
            z_copy(low, 7, 1, half, mate).start()

    def stage_m(i, half):
        for k, start in enumerate((0, 0, FULL - 128)):
            part[i, :, pl.ds(k * HIDE, HIDE)] = dot(toks[i, :, pl.ds(start, FULL)], w_in[k]).astype(BF16)
        core_copy(i).start()

    def stage_c(i, half):
        core_copy(i).wait_recv()

        def add(k, carry):
            quarter = k % 4
            here = mine(quarter, 0, 32)
            there = rows(i * BLOCK + ((y + quarter) % 4) * 32, 32)
            part[i, here] = (part[i, here].astype(F32) + core_in[there].astype(F32)).astype(BF16)
            return carry

        lax.fori_loop(1, 4, add, 0)
        y_raw_copy(i, 0, 2, 0, y_up).start()
        y_raw_copy(i, 1, 2, 1, y_down).start()
        y_raw_copy(i, 2, 1, 1, y_up).start()
        y_raw_copy(i, 3, 3, 0, y_down).start()
        lax.fori_loop(4, 5, add, 0)

    def stage_y1(i, half):
        await_bytes(wide_rows(2 * ROW), y1_r.at[i])
        for side, quarter, device in ((0, 1, y_up), (1, 3, y_down)):
            y_raw[i, side] = (y_raw[i, side].astype(F32) + part[i, mine(quarter, side, ROW)].astype(F32)).astype(BF16)
            y_sum_copy(i, side, device).start()

    def stage_y2(i, half):
        await_bytes(wide_rows(4 * ROW), y2_r.at[i])
        for side, raw in ((0, 3), (1, 2)):
            total = part[i, mine(0, side, ROW)].astype(F32) + y_raw[i, raw].astype(F32) + y_sum[i, side].astype(F32)
            pair[i, side] = total.astype(BF16)
        pair_copy(i).start()

    def activate(i, total):
        gate, up, d_hidden = total[:, :HIDE], total[:, HIDE : 2 * HIDE], total[:, 2 * HIDE :]
        sigmoid = jax.nn.sigmoid(gate)
        activated = gate * sigmoid
        here = mine(0, xh, ROW)
        acts[i, here, pl.ds(0, HIDE)] = (activated * up).astype(BF16)
        acts[i, here, pl.ds(HIDE, HIDE)] = (d_hidden * up * sigmoid * (1.0 + gate * (1.0 - sigmoid))).astype(BF16)
        acts[i, here, pl.ds(2 * HIDE, HIDE)] = (d_hidden * activated).astype(BF16)

    def stage_xn(i, half):
        pair_copy(i).wait_recv()
        activate(i, pair[i, xh].astype(F32) + pair_in[i].astype(F32))

    def stage_x(i, half):
        stage_xn(i, half)
        acts_copy(i, mine(0, xh, ROW), gx_r, across).start()

    cols = (pl.ds(0, CUT), pl.ds(CUT, C - CUT))

    def side_copy(i, k):
        return copy(part.at[i, mine(k, 1 - xh, ROW)], side_in.at[i, k], dp_s.at[i], x_r.at[i], across)

    def raw_cols(i, kind, quarter, cut, device):
        where = cols[cut]
        source = part.at[i, mine(quarter, xh, ROW), where]
        return copy(source, y_raw.at[i, kind, :, where], dp_s.at[i], (y1_r if kind < 2 else y2_r).at[i], device)

    def sum_cols(i, cut, device):
        where = cols[cut]
        return copy(y_raw.at[i, cut, :, where], y_sum.at[i, cut, :, where], dp_s.at[i], y2_r.at[i], device)

    def stage_cx(i, half):
        core_copy(i).wait_recv()

        def add(k, carry):
            here = mine(k, 0, 32)
            there = rows(i * BLOCK + ((y + k) % 4) * 32, 32)
            part[i, here] = (part[i, here].astype(F32) + core_in[there].astype(F32)).astype(BF16)
            side_copy(i, k % 4).start()
            return carry

        lax.fori_loop(2, 6, add, 0)

    def stage_xa(i, half):
        await_bytes(wide_rows(4 * ROW), x_r.at[i])
        for k in (2, 3, 1, 0):
            here = mine(k, xh, ROW)
            part[i, here] = (part[i, here].astype(F32) + side_in[i, k].astype(F32)).astype(BF16)
            if k == 2:
                raw_cols(i, 0, 2, 0, y_up).start()
                raw_cols(i, 1, 2, 1, y_down).start()
            if k == 3:
                raw_cols(i, 3, 3, 0, y_down).start()
            if k == 1:
                raw_cols(i, 2, 1, 1, y_up).start()

    def stage_y1x(i, half):
        await_bytes(wide_rows(ROW), y1_r.at[i])
        for cut, quarter, device in ((0, 1, y_up), (1, 3, y_down)):
            where = cols[cut]
            term = part[i, mine(quarter, xh, ROW), where].astype(F32)
            y_raw[i, cut, :, where] = (y_raw[i, cut, :, where].astype(F32) + term).astype(BF16)
            sum_cols(i, cut, device).start()

    def stage_xxn(i, half):
        await_bytes(wide_rows(2 * ROW), y2_r.at[i])
        terms = [
            part[i, mine(0, xh, ROW), cols[cut]].astype(F32)
            + y_raw[i, raw, :, cols[cut]].astype(F32)
            + y_sum[i, cut, :, cols[cut]].astype(F32)
            for cut, raw in ((0, 3), (1, 2))
        ]
        activate(i, jnp.concatenate(terms, axis=1))

    def stage_xx(i, half):
        stage_xxn(i, half)
        acts_copy(i, mine(0, xh, ROW), gx_r, across).start()

    def g1_cols(i, way, part_no, quarter, device):
        where = (i, mine(quarter, xh, ROW), cols[way ^ part_no])
        return copy(acts.at[where], acts.at[where], dp_s.at[i], (g2_r if part_no else g1_r).at[i], device)

    def g2_cols(i, way, quarter, device):
        where = (i, mine(quarter, xh, ROW), cols[way])
        return copy(acts.at[where], acts.at[where], dp_s.at[i], g2_r.at[i], device)

    def ga_copy(i, quarter):
        return acts_copy(i, mine(quarter, xh, ROW), gx_r, across)

    def stage_ga(i, half):
        for n in range(2):
            g1_cols(i, 0, n, 0, y_up).start()
            g1_cols(i, 1, n, 0, y_down).start()
        ga_copy(i, 0).start()

    def stage_g1x(i, half):
        await_bytes(wide_rows(ROW), g1_r.at[i])
        g2_cols(i, 0, 3, y_up).start()
        g2_cols(i, 1, 1, y_down).start()

    def stage_g2x(i, half):
        await_bytes(wide_rows(2 * ROW), g2_r.at[i])
        for quarter in (3, 1, 2):
            ga_copy(i, quarter).start()

    def stage_g3x(i, half):
        await_bytes(wide_rows(4 * ROW), gx_r.at[i])
        acts_copy(i, rows(core * BLOCK, BLOCK), gc_r, sibling).start()

    def g1_copy(i, part_no, where, device):
        return acts_copy(i, where, g2_r if part_no else g1_r, device)

    def stage_g1(i, half):
        await_bytes(wide_rows(ROW), gx_r.at[i])
        g1_copy(i, 0, mine(0, 0, ROW), y_up).start()
        g1_copy(i, 0, mine(0, 1, ROW), y_down).start()
        g1_copy(i, 1, mine(0, 1, ROW), y_up).start()
        g1_copy(i, 1, mine(0, 0, ROW), y_down).start()
        acts_copy(i, mine(0, 0, 32), gc_r, sibling).start()

    def stage_g2(i, half):
        await_bytes(wide_rows(2 * ROW), g1_r.at[i])
        acts_copy(i, mine(3, 0, ROW), g2_r, y_up).start()
        acts_copy(i, mine(1, 1, ROW), g2_r, y_down).start()

    def stage_g3(i, half):
        await_bytes(wide_rows(4 * ROW), g2_r.at[i])
        for quarter in (3, 1, 2):
            acts_copy(i, mine(quarter, 0, 32), gc_r, sibling).start()

    def stage_g4(i, half):
        await_bytes(wide_rows(BLOCK), gc_r.at[i])
        output = dot(acts[i, :, pl.ds(0, HIDE)], w_out[0])
        d_tokens = dot(acts[i, :, pl.ds(HIDE, HIDE)], w_out[1]) + dot(acts[i, :, pl.ds(2 * HIDE, HIDE)], w_out[2])
        outs[i, :, pl.ds(0, FULL - 128)] = output[:, : FULL - 128].astype(BF16)
        outs[i, :, pl.ds(FULL - 128, 128)] = (output[:, FULL - 128 :] + d_tokens[:, :128]).astype(BF16)
        outs[i, :, pl.ds(FULL, FULL - 128)] = d_tokens[:, 128:].astype(BF16)

    def stage_w(i, half):
        left = toks[i, :, pl.ds(0, FULL)].T[:WIDE]
        grads[0] += dot(left, acts[i, :, pl.ds(HIDE, HIDE)])
        grads[1] += dot(left, acts[i, :, pl.ds(2 * HIDE, HIDE)])
        left = toks[i, :, pl.ds(FULL - 128, FULL)].T[EDGE:]
        grads[2] += dot(left, acts[i, :, pl.ds(0, HIDE)])

    def stage_k(i, half):
        p, hr = i % 4, i // 4
        step = 3 - p
        ahead, behind = outs.at[i, rows(half * CHAIN_ROWS, CHAIN_ROWS)], outs.at[i, rows(BLOCK + half * CHAIN_ROWS, CHAIN_ROWS)]

        @pl.when(p == 3)
        def _():
            @pl.when(hr == 0)
            def _():
                chain_copy(behind, 0, 0, 0, half, z_up).start()

            @pl.when(hr == 1)
            def _():
                chain_copy(behind, 1, 1, 0, half, z_down).start()

        @pl.when(p < 3)
        def _():
            @pl.when(p == 2)
            def _():
                await_bytes(chain_in.at[hr, 0, 0, half], k_r.at[hr, 0, half])

            @pl.when(p < 2)
            def _():
                await_bytes(toks.at[0, rows(0, 2 * CHAIN_ROWS)], k_r.at[hr, step - 1, half])

            for way, block, device in ((0, ahead, z_up), (1, behind, z_down)):
                @pl.when((step > 1) | (hr == way))
                def _():
                    block[...] = (block[...].astype(F32) + chain_in[hr, way, step - 1, half].astype(F32)).astype(BF16)

                chain_copy(block, hr, way, step, half, device).start()

    def stage_ki(hr, half):
        here = rows(half * CHAIN_ROWS, CHAIN_ROWS)
        block = outs.at[hr * 4 + 3, here]
        await_bytes(toks.at[0, rows(0, 2 * CHAIN_ROWS)], k_r.at[hr, 3, half])
        total = block[...].astype(F32) + chain_in[hr, 0, 3, half].astype(F32) + chain_in[hr, 1, 3, half].astype(F32)
        block[...] = total.astype(BF16)

        @pl.when(hr == 0)
        def _():
            first[here] = total

        @pl.when(hr == 1)
        def _():
            last_copy(half).start()

    def stage_s(i, half):
        @pl.when(i == 3)
        def _():
            await_bytes(toks.at[i, rows(0, BLOCK)], z_s.at[i])

        @pl.when(i != 3)
        def _():
            await_bytes(toks.at[i], z_s.at[i])

        await_bytes(wide_rows(30 * ROW), dp_s.at[i])

    def store(k):
        return pltpu.make_async_copy(grads.at[k], grads_hbm.at[k], store_sem.at[k])

    def stage_go(i, half):
        @pl.when(i == 0)
        def _():
            for k in range(3):
                store(k).start()

    barrier = pltpu.get_barrier_semaphore()
    peers = (sibling, y_up, y_down, across, mate, z_up, z_down)
    for device in peers:
        pl.semaphore_signal(barrier, inc=1, device_id=device, device_id_type=MESH)
    features = [
        pltpu.make_async_copy(ref, features_t.at[pl.ds(k * WIDE, WIDE)], load_sem.at[3 + k])
        for k, ref in enumerate((tokens_hbm, cotangent_hbm))
    ]
    loads = [
        pltpu.make_async_copy(ref, codes.at[k], load_sem.at[k]) for k, ref in enumerate((gate_hbm, up_hbm, down_hbm))
    ]
    for load in features + loads:
        load.start()
    for load in features:
        load.wait()
    own[...] = features_t[...].T
    pl.semaphore_wait(barrier, len(peers))

    for half in range(Z_PARTS):
        z_copy(own_half(half), 0, 1, half, z_up).start()
        z_copy(own_half(half), 0, 0, half, z_down).start()
        xl_copy(half).start()
    toks[3, rows(0, BLOCK)] = own[...]

    zeros = jnp.zeros((EDGE, HIDE), BF16)
    grads[...] = jnp.zeros_like(grads)
    loads[0].wait()
    w_gate = (codes[0].astype(F32) * gate_scale[...].reshape(1, HIDE)).astype(BF16)
    w_in[0, :WIDE] = w_gate
    w_in[0, WIDE:] = zeros
    w_out[1] = jnp.concatenate((zeros, w_gate), axis=0).T
    loads[1].wait()
    w_up = (codes[1].astype(F32) * up_scale[...].reshape(1, HIDE)).astype(BF16)
    w_in[1, :WIDE] = w_up
    w_in[1, WIDE:] = zeros
    w_out[2] = jnp.concatenate((zeros, w_up), axis=0).T
    loads[2].wait()
    w_down_t = (codes[2].astype(F32) * down_scale[...].reshape(WIDE, 1)).astype(BF16)
    w_in[2, :EDGE] = zeros
    w_in[2, EDGE:] = w_down_t
    w_out[0] = jnp.concatenate((w_down_t, zeros), axis=0).T

    stages = (
        stage_xl, stage_z, stage_m, stage_c, stage_y1, stage_y2, stage_x, stage_g1, stage_g2, stage_g3, stage_g4,
        stage_w, stage_k, stage_ki, stage_s, stage_go, stage_cx, stage_xa, stage_y1x, stage_xx, stage_xn, stage_xxn, stage_ga,
        stage_g1x, stage_g2x, stage_g3x,
    )

    steps = [KINDS.index(kind) * 32 + half * 8 + i for kind, i, half in ORDER]
    steps += [KINDS.index("GO") * 32 + 1] * (-len(steps) % 3)
    words = [sum(code << (10 * k) for k, code in enumerate(steps[n : n + 3])) for n in range(0, len(steps), 3)]

    def dispatch(low, high, kind, i, half):
        if high - low == 1:
            stages[low](i, half)
            return
        middle = (low + high) // 2

        @pl.when(kind < middle)
        def _():
            dispatch(low, middle, kind, i, half)

        @pl.when(kind >= middle)
        def _():
            dispatch(middle, high, kind, i, half)

    def step(k, word):
        dispatch(0, len(stages), word // 32 % 32, word % 8, word // 8 % 4)
        return word // 1024

    def three_steps(n, carry):
        word = jnp.int32(words[0])
        for k in range(1, len(words)):
            word = jnp.where(n == k, words[k], word)
        lax.fori_loop(0, 3, step, word)
        return carry

    lax.fori_loop(0, len(words), three_steps, 0)

    await_bytes(last_in, f_r.at[0])
    total = (first[...] + last_in[...].reshape(BLOCK, 2 * WIDE).astype(F32)).astype(BF16).T
    output_t[...] = total[:WIDE]
    d_tokens_t[...] = total[WIDE:]

    await_bytes(toks.at[pl.ds(0, 7)], k_s.at[0])
    await_bytes(last_in, f_s.at[0])
    for k in range(3):
        store(k).wait()


def settle(output_in, d_tokens_in, grads_in, output_t, d_tokens_t, grad_gate, grad_up, grad_down_t, edges, held, sems):
    pairs = [(output_in, edges.at[0], output_t), (d_tokens_in, edges.at[1], d_tokens_t)]
    pairs += [(grads_in.at[k], held.at[k], grad) for k, grad in enumerate((grad_gate, grad_up, grad_down_t))]
    loads = [pltpu.make_async_copy(a, b, sems.at[0, k]) for k, (a, b, _) in enumerate(pairs)]
    stores = [pltpu.make_async_copy(b, c, sems.at[1, k]) for k, (_, b, c) in enumerate(pairs)]
    for one in loads:
        one.start()
    for load, one in zip(loads, stores):
        load.wait()
        one.start()
    for one in stores:
        one.wait()


def local(tokens, cotangent, gate_codes, gate_scale, up_codes, up_scale, down_codes, down_scale):
    vmem = pl.BlockSpec(memory_space=pltpu.VMEM)
    dma = pltpu.SemaphoreType.DMA
    anywhere = pl.BlockSpec(memory_space=pl.ANY)
    edge = jax.ShapeDtypeStruct((WIDE, BLOCK), BF16)
    results = pl.pallas_call(
        kernel,
        out_shape=(edge, edge, jax.ShapeDtypeStruct((3, WIDE, HIDE), F32)),
        in_specs=[anywhere, anywhere, anywhere, vmem, anywhere, vmem, anywhere, vmem],
        out_specs=(vmem, vmem, anywhere),
        scratch_shapes=[
            pltpu.VMEM((2 * WIDE, BLOCK), BF16),
            pltpu.VMEM((3, WIDE, HIDE), BF16),
            pltpu.VMEM((3, WIDE, HIDE), F32),
            dma((5,)),
            dma((3,)),
            pltpu.VMEM((BLOCK, 2 * WIDE), BF16),
            pltpu.VMEM((UNITS, UNIT, 2 * WIDE), BF16),
            pltpu.VMEM((3, FULL, HIDE), BF16),
            pltpu.VMEM((3, HIDE, FULL), BF16),
            pltpu.VMEM((UNITS, UNIT, C), BF16),
            pltpu.VMEM((UNITS * BLOCK, C), BF16),
            pltpu.VMEM((UNITS, 4, ROW, C), BF16),
            pltpu.VMEM((UNITS, 2, ROW, C), BF16),
            pltpu.VMEM((UNITS, 2, ROW, C), BF16),
            pltpu.VMEM((UNITS, ROW, C), BF16),
            pltpu.VMEM((UNITS, UNIT, C), BF16),
            pltpu.VMEM((UNITS, UNIT, 2 * WIDE), BF16),
            pltpu.VMEM((2, 2, 4, CHAIN_PARTS, CHAIN_ROWS, 2 * WIDE), BF16),
            pltpu.VMEM((BLOCK, 2 * WIDE), F32),
            pltpu.VMEM((CHAIN_PARTS, CHAIN_ROWS, 2 * WIDE), BF16),
            pltpu.VMEM((UNITS, 4, ROW, C), BF16),
            dma((UNITS,)),
            dma((UNITS,)),
            dma((1,)),
            dma((1,)),
            dma((UNITS, Z_PARTS)),
            dma((Z_PARTS,)),
            *[dma((UNITS,))] * 8,
            dma((2, 4, CHAIN_PARTS)),
            dma((1,)),
        ],
        compiler_params=pltpu.CompilerParams(
            collective_id=0, has_side_effects=True, vmem_limit_bytes=64 * 1024 * 1024 - 256 * 1024
        ),
    )(
        tokens.T, cotangent.T, gate_codes, gate_scale, up_codes, up_scale, down_codes.T, down_scale.reshape(WIDE)
    )
    grad = jax.ShapeDtypeStruct((WIDE, HIDE), F32)
    output_t, d_tokens_t, grad_gate, grad_up, grad_down_t = pl.pallas_call(
        settle,
        out_shape=(edge, edge, grad, grad, grad),
        in_specs=[anywhere] * 3,
        out_specs=(anywhere,) * 5,
        scratch_shapes=[pltpu.VMEM((2, WIDE, BLOCK), BF16), pltpu.VMEM((3, WIDE, HIDE), F32), dma((2, 5))],
        compiler_params=pltpu.CompilerParams(vmem_limit_bytes=60 * 1024 * 1024),
    )(*results)
    return output_t.T, d_tokens_t.T, grad_gate, grad_up, grad_down_t.T


def solution(mesh):
    placed = (
        P("fsdp", "dp"),
        P("fsdp", "dp"),
        P("dp", "fsdp"),
        P("fsdp"),
        P("dp", "fsdp"),
        P("fsdp"),
        P("fsdp", "dp"),
        P(None, "dp"),
    )
    return jax.shard_map(
        local,
        mesh=mesh,
        in_specs=placed,
        out_specs=(
            P("fsdp", "dp"),
            P("fsdp", "dp"),
            P("dp", "fsdp"),
            P("dp", "fsdp"),
            P("fsdp", "dp"),
        ),
        check_vma=False,
    )
```

time: 128 us -> 125 us (0.977)
  Pallas kernels: 128 us -> 125 us
    pallas_call x1, Pallas kernels: 124 us -> 121 us  [local(): pl.pallas_call(kernel, out_shape=(edge, edge, jax.ShapeDtypeStruct((3, WI...]
where the time goes in v3:
time: 125 us
  Pallas kernels  125 us (100%)
    pallas_call x1, Pallas kernels, local(): pl.pallas_call(kernel, out_shape=(edge, edge, jax.ShapeDtypeStruct((3, WI...  121 us
    pallas_call x1, Pallas kernels, local(): pl.pallas_call(settle, out_shape=(edge, edge, grad, grad, grad), in_specs...  4.01 us

profile of v3, /device:TPU:1, one launch (start us, length us, event | category | flops | bytes accessed | tf_op | source)
XLA Modules:
  0.0 125.2 jit_solution(3723886875675765910)
XLA Ops:
  0.6 120.5 %shard_map.119 = (bf16[448,128]{1,0:T(8,128)(2,1)}, bf16[448,128]{1,0:T(8,128)(2,1)}, f32[3,448,896]{2,1,0:T(8,128)}) custom-call(bf16[448,128]{1,0:T(8,128)(2,1)} %bitcast.8, bf16[448,128]{1,0:T(8,128)(2,1)} %bitcast.9, bf16[448,896]{1,0:T(8,128)(2,1)} %gate_hbm.1, f32[896]{0:T(1024)} %gate_scale.1, bf16[448,896]{1,0:T(8,128)(2,1)} %up_hbm.1, ...), custom_call_target="tpu_custom_call" | custom-call | tf_op jit(solution)/shard_map/pallas_call | solution.py:515
  121.2 4.0 %shard_map.120 = (bf16[448,128]{1,0:T(8,128)(2,1)}, bf16[448,128]{1,0:T(8,128)(2,1)}, f32[448,896]{1,0:T(8,128)}, f32[448,896]{1,0:T(8,128)}, f32[448,896]{1,0:T(8,128)}) custom-call(bf16[448,128]{1,0:T(8,128)(2,1)} %get-tuple-element.13.output_in, bf16[448,128]{1,0:T(8,128)(2,1)} %get-tuple-element.14.d_tokens_in, f32[3,448,896]{2,1,0:T(8,128)} %get-tuple-element.15.grads_in), custom_call_target="tpu_custom_call" | custom-call | tf_op jit(solution)/shard_map/pallas_call | solution.py:559

commit v4 on v3

--- a/solution.py
+++ b/solution.py
@@ -451,36 +451,8 @@
         stage_g1x, stage_g2x, stage_g3x,
     )
 
-    steps = [KINDS.index(kind) * 32 + half * 8 + i for kind, i, half in ORDER]
-    steps += [KINDS.index("GO") * 32 + 1] * (-len(steps) % 3)
-    words = [sum(code << (10 * k) for k, code in enumerate(steps[n : n + 3])) for n in range(0, len(steps), 3)]
-
-    def dispatch(low, high, kind, i, half):
-        if high - low == 1:
-            stages[low](i, half)
-            return
-        middle = (low + high) // 2
-
-        @pl.when(kind < middle)
-        def _():
-            dispatch(low, middle, kind, i, half)
-
-        @pl.when(kind >= middle)
-        def _():
-            dispatch(middle, high, kind, i, half)
-
-    def step(k, word):
-        dispatch(0, len(stages), word // 32 % 32, word % 8, word // 8 % 4)
-        return word // 1024
-
-    def three_steps(n, carry):
-        word = jnp.int32(words[0])
-        for k in range(1, len(words)):
-            word = jnp.where(n == k, words[k], word)
-        lax.fori_loop(0, 3, step, word)
-        return carry
-
-    lax.fori_loop(0, len(words), three_steps, 0)
+    for kind, i, half in ORDER:
+        stages[KINDS.index(kind)](i, half)
 
     await_bytes(last_in, f_r.at[0])
     total = (first[...] + last_in[...].reshape(BLOCK, 2 * WIDE).astype(F32)).astype(BF16).T

time: 125 us -> 125 us (level)
  no operation moved by 1% of the time
where the time goes in v4:
time: 125 us; the launch traced here: 124 us
  Pallas kernels  124 us (99%)
    pallas_call x1, Pallas kernels, local(): pl.pallas_call(kernel, out_shape=(edge, edge, jax.ShapeDtypeStruct((3, WI...  120 us
    pallas_call x1, Pallas kernels, local(): pl.pallas_call(settle, out_shape=(edge, edge, grad, grad, grad), in_specs...  4.01 us

profile of v4, /device:TPU:1, one launch (start us, length us, event | category | flops | bytes accessed | tf_op | source)
XLA Modules:
  0.0 124.4 jit_solution(2590268328839103406)
XLA Ops:
  0.6 119.6 %shard_map.119 = (bf16[448,128]{1,0:T(8,128)(2,1)}, bf16[448,128]{1,0:T(8,128)(2,1)}, f32[3,448,896]{2,1,0:T(8,128)}) custom-call(bf16[448,128]{1,0:T(8,128)(2,1)} %bitcast.8, bf16[448,128]{1,0:T(8,128)(2,1)} %bitcast.9, bf16[448,896]{1,0:T(8,128)(2,1)} %gate_hbm.1, f32[896]{0:T(1024)} %gate_scale.1, bf16[448,896]{1,0:T(8,128)(2,1)} %up_hbm.1, ...), custom_call_target="tpu_custom_call" | custom-call | tf_op jit(solution)/shard_map/pallas_call | solution.py:487
  120.2 4.0 %shard_map.120 = (bf16[448,128]{1,0:T(8,128)(2,1)}, bf16[448,128]{1,0:T(8,128)(2,1)}, f32[448,896]{1,0:T(8,128)}, f32[448,896]{1,0:T(8,128)}, f32[448,896]{1,0:T(8,128)}) custom-call(bf16[448,128]{1,0:T(8,128)(2,1)} %get-tuple-element.13.output_in, bf16[448,128]{1,0:T(8,128)(2,1)} %get-tuple-element.14.d_tokens_in, f32[3,448,896]{2,1,0:T(8,128)} %get-tuple-element.15.grads_in), custom_call_target="tpu_custom_call" | custom-call | tf_op jit(solution)/shard_map/pallas_call | solution.py:531
